TPU v7x, 512 devices: a whole 4x4x16 slice. The times are simulated.
512 devices in a mesh: band: 16 (over y, x_hi, core), pencil: 32 (over x_lo, z).
Axes of the slice: x: 4 (x_hi: 2, x_lo: 2; x = x_hi * 2 + x_lo), y: 4, z: 16, core: 2. Of those that a mesh axis runs over, the one named last changes fastest.
Arguments:
- panels: bfloat16 [1024, 96, 8, 128], P('band', 'pencil'), may hold values from -7 to 7
- potential: float32 [96, 8, 128], P('pencil'), may hold values from -1 to 1
- plan: int32 [16], replicated, may hold values from 0 to 15, each once
Outputs:
- projected: bfloat16 [1024, 96, 8, 128], P('band', 'pencil')
Inputs may be any that keep to these rules, and one draw needn't show every extreme that they name: `plan`: each band group's turn appears once.
All inputs are finite; a program needn't handle non-finite values.
Results may differ from a plain program's by a relative error of at most 0.009.
Values may be sent and summed in bfloat16 or wider, within the bound.
No kernel may reach another device: no remote copies, remote signals or barrier semaphores. Data moves between devices by JAX's collectives and lax.ppermute only.
A program may use at most 64 MiB of HBM per device.

v0:
```python
import jax
import jax.numpy as jnp
from jax import lax
from jax.sharding import PartitionSpec as P

WEIGHTS = (-49.0 / 18.0, 1.5, -0.15, 1.0 / 90.0)
CENTRE = 6.05
HALFWIDTH = 4.05


def extended_2(shard, sides, width):
    for axis, dim in sides:
        size, length = (lax.axis_size(axis), shard.shape[dim])
        up = [(i, (i + 1) % size) for i in range(size)]
        down = [(j, i) for i, j in up]
        last = lax.slice_in_dim(shard, length - width, length, axis=dim)
        initial = lax.slice_in_dim(shard, 0, width, axis=dim)
        before = lax.ppermute(last, axis, up)
        after = lax.ppermute(initial, axis, down)
        shard = jnp.concatenate([before, shard, after], axis=dim)
    return shard


def hamiltonian(field_low, potential):
    extended = extended_2(field_low, (("pencil", 1),), 3)
    field = field_low.astype(jnp.float32)
    planes = field.shape[1]
    total = 3.0 * WEIGHTS[0] * field
    for dist in range(1, 4):
        upper = extended[:, 3 + dist : 3 + dist + planes].astype(jnp.float32)
        lower = extended[:, 3 - dist : 3 - dist + planes].astype(jnp.float32)
        total = total + WEIGHTS[dist] * (upper + lower)
        for axis in (2, 3):
            ahead = jnp.roll(field_low, dist, axis).astype(jnp.float32)
            behind = jnp.roll(field_low, -dist, axis).astype(jnp.float32)
            total = total + WEIGHTS[dist] * (ahead + behind)
    return (field, -0.5 * total + potential[None] * field)


def body(panels, potential, plan):
    start, applied = hamiltonian(panels, potential)
    first = ((applied - CENTRE * start) / HALFWIDTH).astype(jnp.bfloat16)
    firstf, applied_two = hamiltonian(first, potential)
    filtered = (2.0 * (applied_two - CENTRE * firstf) / HALFWIDTH - start).astype(jnp.bfloat16)
    orbitals = panels.shape[0]
    local_rows = panels.reshape(orbitals, -1)
    local_filtered = filtered.reshape(orbitals, -1)
    scale = 1.0 / (local_rows.shape[1] * lax.axis_size("pencil"))
    gathered = lax.all_gather(local_rows, "band", axis=0, tiled=True)
    partial_sums = lax.dot_general(
        gathered, local_filtered, (((1,), (1,)), ((), ())), preferred_element_type=jnp.float32
    )
    turn = plan[lax.axis_index("band")]
    before = jnp.repeat(plan < turn, orbitals, total_repeat_length=gathered.shape[0])
    summed = lax.psum(partial_sums.astype(jnp.bfloat16), "pencil").astype(jnp.float32)
    coef = jnp.where(before[:, None], summed * scale, 0.0).astype(jnp.bfloat16)
    removed = lax.dot_general(
        coef, gathered, (((0,), (0,)), ((), ())), preferred_element_type=jnp.float32
    )
    result = (local_filtered.astype(jnp.float32) - removed).astype(jnp.bfloat16)
    return result.reshape(panels.shape)


def solution(mesh):
    in_specs = (P("band", "pencil", None, None), P("pencil", None, None), P())
    out_specs = P("band", "pencil", None, None)
    return jax.shard_map(body, mesh=mesh, in_specs=in_specs, out_specs=out_specs, check_vma=False)
```

profile of v0, /device:TPU:24, one launch (start us, length us, event | category | flops | bytes accessed | tf_op | source)
XLA Modules:
  0.0 364.1 jit_solution(1367218037311266784)
XLA Ops:
  6.5 1.9 copy.13
  8.4 0.0 all-gather.2.cloned.1.call-update
  8.4 0.0 all-reduce.2.cloned.1.call-start
  8.5 3.8 %collective-permute-start.1 = (bf16[64,3,8,128]{3,2,1,0:T(8,128)(2,1)}, bf16[64,3,8,128]{3,2,1,0:T(8,128)(2,1)S(1)}, u32[]{:S(2)}, u32[]{:S(2)}) collective-permute-start(bf16[64,3,8,128]{3,2,1,0:T(8,128)(2,1)} %param.5), channel_id=1, source_target_pairs={{0,1},{1,2},{2,3},{3,4},{4,5},{5,6},{6,7},{7,8},{8,9},{9,10},{10,1... | collective-permute-start | bytes 1179656 | tf_op jit(solution)/shard_map/ppermute | solution.py:18
  12.3 10.4 %collective-permute-start = (bf16[64,3,8,128]{3,2,1,0:T(8,128)(2,1)}, bf16[64,3,8,128]{3,2,1,0:T(8,128)(2,1)S(1)}, u32[]{:S(2)}, u32[]{:S(2)}) collective-permute-start(bf16[64,3,8,128]{3,2,1,0:T(8,128)(2,1)} %param.5), channel_id=1, source_target_pairs={{1,0},{2,1},{3,2},{4,3},{5,4},{6,5},{7,6},{8,7},{9,8},{10,9},{11,1... | collective-permute-start | bytes 1179656 | tf_op jit(solution)/shard_map/ppermute | solution.py:19
  22.8 1.3 dynamic_slice.3
  24.0 0.8 add_add_fusion.1
  24.8 1.3 fusion.59
  26.1 1.3 fusion.63
  27.3 1.3 fusion.55
  28.6 1.3 fusion.52
  29.9 1.3 fusion.53
  31.2 0.2 fusion.54
  31.4 0.2 fusion.56
  31.6 0.2 fusion.57
  31.8 0.2 fusion.58
  31.9 0.2 fusion.60
  32.1 0.2 fusion.61
  32.3 0.2 fusion.62
  32.5 0.6 broadcast_compare_fusion
  33.1 0.7 fusion.64
  33.8 4.5 %select_reduce_fusion = (pred[1024]{0:T(1024)(128)(4,1)S(1)}, pred[1024]{0:T(1024)(128)(4,1)S(1)}, pred[1024]{0:T(1024)(128)(4,1)S(1)}, pred[1024]{0:T(1024)(128...) fusion(pred[]{:T(512)} %bitcast.14, ...), kind=kLoop, calls=%fused_computation.56 | loop fusion | flops 23552 | bytes 18439 | tf_op jit(solution)/shard_map/jit(_take)/gather | solution.py:54
  38.4 0.1 constant_dynamic-update-slice_fusion.1
  38.6 0.1 constant_dynamic-update-slice_fusion
  38.7 3.8 %fusion.29 = bf16[64,3,8,128]{3,2,1,0:T(8,128)(2,1)S(1)} fusion(bf16[64,3,8,128]{3,2,1,0:T(8,128)(2,1)S(1)} %collective-permute-done.1, bf16[64,3,8,128]{3,2,1,0:T(8,128)(2,1)S(1)} %collective-permute-done, bf16[64,3,8,128]{3,2,1,0:T(8,128)(2,1)S(1)} %copy-done, bf16[64,6,8,128]{3,2,1,0:T(8,128)(2,1)S(1)} %get-tuple-element.76, ...), kind=kLoop, calls=%fused_computation.42 | loop fusion | flops 17694720 | bytes 7876608 | tf_op jit(solution)/shard_map/convert_element_type | solution.py:42
  42.5 3.9 %collective-permute-start.2 = (bf16[64,3,8,128]{3,2,1,0:T(8,128)(2,1)S(1)}, bf16[64,3,8,128]{3,2,1,0:T(8,128)(2,1)S(1)}, u32[]{:S(2)}, u32[]{:S(2)}) collective-permute-start(bf16[64,3,8,128]{3,2,1,0:T(8,128)(2,1)S(1)} %fusion.29), channel_id=1, source_target_pairs={{1,0},{2,1},{3,2},{4,3},{5,4},{6,5},{7,6},{8,7},{9,8},{10,9},{11,1... | collective-permute-start | bytes 1179656 | tf_op jit(solution)/shard_map/ppermute | solution.py:19
  46.4 2.1 collective-permute-start.3
  48.5 0.1 fusion.47
  48.6 0.1 fusion.43
  48.8 0.2 fusion.40
  49.0 0.2 fusion.41
  49.1 0.2 fusion.42
  49.3 0.2 fusion.44
  49.5 0.2 fusion.45
  49.7 0.2 fusion.46
  49.8 0.2 fusion.48
  50.0 0.2 fusion.49
  50.2 0.1 fusion.51
  50.3 0.2 fusion.50
  50.5 4.4 %collective-permute-done.2 = bf16[64,3,8,128]{3,2,1,0:T(8,128)(2,1)S(1)} collective-permute-done((bf16[64,3,8,128]{3,2,1,0:T(8,128)(2,1)S(1)}, bf16[64,3,8,128]{3,2,1,0:T(8,128)(2,1)S(1)}, u32[]{:S(2)}, u32[]{:S(2)}) %collective-permute-start.2) | collective-permute-done | bytes 393248 | tf_op jit(solution)/shard_map/ppermute | solution.py:19
  54.9 5.5 %collective-permute-done.3 = bf16[64,3,8,128]{3,2,1,0:T(8,128)(2,1)S(1)} collective-permute-done((bf16[64,3,8,128]{3,2,1,0:T(8,128)(2,1)S(1)}, bf16[64,3,8,128]{3,2,1,0:T(8,128)(2,1)S(1)}, u32[]{:S(2)}, u32[]{:S(2)}) %collective-permute-start.3) | collective-permute-done | bytes 393248 | tf_op jit(solution)/shard_map/ppermute | solution.py:18
  60.4 3.7 %fusion.30 = bf16[64,3,8,128]{3,2,1,0:T(8,128)(2,1)S(1)} fusion(bf16[64,3,8,128]{3,2,1,0:T(8,128)(2,1)S(1)} %copy-done, bf16[64,3,8,128]{3,2,1,0:T(8,128)(2,1)S(1)} %collective-permute-done.3, bf16[64,3,8,128]{3,2,1,0:T(8,128)(2,1)S(1)} %collective-permute-done.2, bf16[64,3,8,128]{3,2,1,0:T(8,128)(2,1)S(1)} %fusion.29, ...), kind=kLoop, calls=%fused_computation.43 | loop fusion | flops 20447232 | bytes 6696960 | tf_op jit(solution)/shard_map/convert_element_type | solution.py:44
  64.1 28.3 %all-gather.2.cloned.1.call-done = bf16[1024,3072]{1,0:T(8,128)(2,1)} async-done(((bf16[64,3072]{1,0:T(8,128)(2,1)}), bf16[1024,3072]{1,0:T(8,128)(2,1)}) %all-gather.2.cloned.1.call-update) | async-done | bytes 6291472 | tf_op jit(solution)/shard_map/all_gather | solution.py:49
  92.4 5.3 %fusion.2 = bf16[1024,64]{1,0:T(8,128)(2,1)} fusion(bf16[1024,3072]{1,0:T(8,128)(2,1)} %all-gather.2.cloned.1.call-done, bf16[8,8,24,128]{3,2,1,0:T(8,128)(2,1)S(1)} %bitcast.47), kind=kOutput, calls=%fused_computation.11 | convolution fusion | flops 402718720 | bytes 6815744 | tf_op jit(solution)/shard_map/dot_general | solution.py:50
  97.7 5.7 %select_select_fusion = pred[1024]{0:T(1024)(128)(4,1)S(1)} fusion(pred[1024]{0:T(1024)(128)(4,1)S(1)} %get-tuple-element.26, pred[1024]{0:T(1024)(128)(4,1)S(1)} %get-tuple-element.25, pred[1024]{0:T(1024)(128)(4,1)S(1)} %get-tuple-element.20, pred[1024]{0:T(1024)(128)(4,1)S(1)} %get-tuple-element.21, pred[1024]{0:T(1024)(128)(4,1)S(1)} %get-tuple-element.22, ...), kind=kLoop, calls=%fused_computation.73 | loop fusion | flops 18432 | bytes 15401 | tf_op jit(solution)/shard_map/jit(_take)/select_n | solution.py:54
  103.5 248.7 %all-reduce.2.cloned.1.call-done = bf16[1024,64]{1,0:T(8,128)(2,1)} async-done(((bf16[1024,64]{1,0:T(8,128)(2,1)}), bf16[1024,64]{1,0:T(8,128)(2,1)}) %all-reduce.2.cloned.1.call-update) | async-done | bytes 131088 | tf_op jit(solution)/shard_map/psum | solution.py:55
  352.2 4.2 %fusion.1 = bf16[8,8,24,128]{3,1,2,0:T(8,128)(2,1)S(1)} fusion(bf16[1024,3072]{1,0:T(8,128)(2,1)} %all-gather.2.cloned.1.call-done, bf16[8,8,24,128]{3,2,1,0:T(8,128)(2,1)S(1)} %bitcast.48, bf16[1024,64]{1,0:T(8,128)(2,1)} %all-reduce.2.cloned.1.call-done, pred[1024]{0:T(1024)(128)(4,1)S(1)} %select_select_fusion), kind=kOutput, calls=%fused_computation.6 | convolution fusion | flops 403505152 | bytes 7209984 | tf_op jit(solution)/shard_map/dot_general | solution.py:57
  356.4 0.8 copy.6
  (14 shorter events, 0.1 us)
Async XLA Ops:
  6.5 24.7 %copy-start = (bf16[64,3,8,128]{3,2,1,0:T(8,128)(2,1)S(1)}, bf16[64,3,8,128]{3,2,1,0:T(8,128)(2,1)}, u32[]{:S(2)}) copy-start(bf16[64,3,8,128]{3,2,1,0:T(8,128)(2,1)} %param.5) | copy-start | bytes 1179652
  6.5 85.9 %all-gather.2.cloned.1.call-start = ((), (), s32[]{:S(2)}) async-start(), calls=%async_computation | async-start | bytes 6684672 | tf_op jit(solution)/shard_map/all_gather | solution.py:49
  8.4 343.7 %all-reduce.2.cloned.1.call-start = ((), (), s32[]{:S(2)}) async-start(), calls=%async_computation.1 | async-start | bytes 524288 | tf_op jit(solution)/shard_map/psum | solution.py:55
  8.5 29.9 %collective-permute-start.1 = (bf16[64,3,8,128]{3,2,1,0:T(8,128)(2,1)}, bf16[64,3,8,128]{3,2,1,0:T(8,128)(2,1)S(1)}, u32[]{:S(2)}, u32[]{:S(2)}) collective-permute-start(bf16[64,3,8,128]{3,2,1,0:T(8,128)(2,1)} %param.5), channel_id=1, source_target_pairs={{0,1},{1,2},{2,3},{3,4},{4,5},{5,6},{6,7},{7,8},{8,9},{9,10},{10,1... | collective-permute-start | bytes 1179656 | tf_op jit(solution)/shard_map/ppermute | solution.py:18
  12.3 26.3 %collective-permute-start = (bf16[64,3,8,128]{3,2,1,0:T(8,128)(2,1)}, bf16[64,3,8,128]{3,2,1,0:T(8,128)(2,1)S(1)}, u32[]{:S(2)}, u32[]{:S(2)}) collective-permute-start(bf16[64,3,8,128]{3,2,1,0:T(8,128)(2,1)} %param.5), channel_id=1, source_target_pairs={{1,0},{2,1},{3,2},{4,3},{5,4},{6,5},{7,6},{8,7},{9,8},{10,9},{11,1... | collective-permute-start | bytes 1179656 | tf_op jit(solution)/shard_map/ppermute | solution.py:19
  29.9 2.5 copy-start.3
  31.4 7.3 %copy-start.1 = (f32[3,8,128]{2,1,0:T(8,128)S(1)}, f32[3,8,128]{2,1,0:T(8,128)}, u32[]{:S(2)}) copy-start(f32[3,8,128]{2,1,0:T(8,128)} %param.6) | copy-start | bytes 36868
  42.5 12.5 %collective-permute-start.2 = (bf16[64,3,8,128]{3,2,1,0:T(8,128)(2,1)S(1)}, bf16[64,3,8,128]{3,2,1,0:T(8,128)(2,1)S(1)}, u32[]{:S(2)}, u32[]{:S(2)}) collective-permute-start(bf16[64,3,8,128]{3,2,1,0:T(8,128)(2,1)S(1)} %fusion.29), channel_id=1, source_target_pairs={{1,0},{2,1},{3,2},{4,3},{5,4},{6,5},{7,6},{8,7},{9,8},{10,9},{11,1... | collective-permute-start | bytes 1179656 | tf_op jit(solution)/shard_map/ppermute | solution.py:19
  46.4 14.0 %collective-permute-start.3 = (bf16[64,3,8,128]{3,2,1,0:T(8,128)(2,1)S(1)}, bf16[64,3,8,128]{3,2,1,0:T(8,128)(2,1)S(1)}, u32[]{:S(2)}, u32[]{:S(2)}) collective-permute-start(bf16[64,3,8,128]{3,2,1,0:T(8,128)(2,1)S(1)} %fusion.29), channel_id=1, source_target_pairs={{0,1},{1,2},{2,3},{3,4},{4,5},{5,6},{6,7},{7,8},{8,9},{9,10},{10,1... | collective-permute-start | bytes 1179656 | tf_op jit(solution)/shard_map/ppermute | solution.py:18
  60.4 37.3 %copy-start.2 = (s32[8,128]{1,0:T(8,128)S(1)}, s32[8,128]{1,0:T(8,128)}, u32[]{:S(2)}) copy-start(s32[8,128]{1,0:T(8,128)} %constant.109.clone.1) | copy-start | bytes 12292
Sparse Core Ops, SparseCore 0:
  10.7 81.6 all-gather.1
  97.8 254.2 all-reduce.1
where the time goes:
time: 365 us; the launch traced here: 364 us
  waiting for transfers between devices  287 us (79%)
  starting transfers between devices  20.3 us (6%)
  other arithmetic  19.2 us (5%)
  local copies, waits for them, and re-layouts  14.4 us (4%)
  between operations  13.7 us (4%)
  matrix products  9.47 us (3%)
    psum x1, waiting for transfers between devices, body(): lax.psum(partial_sums.astype(jnp.bfloat16), 'pencil').astype(jnp.float32)  249 us
    all_gather x1, waiting for transfers between devices, body(): gathered = lax.all_gather(local_rows, 'band', axis=0, tiled=True)  28.3 us
    ppermute x2, starting transfers between devices, extended_2(): after = lax.ppermute(initial, axis, down)  14.4 us
    slice x24, local copies, waits for them, and re-layouts, hamiltonian(): behind = jnp.roll(field_low, -dist, axis).astype(jnp.float32)  9.46 us
  transfers between devices with their start and end apart: 6, of which 4 were waited for; matrix products, arithmetic and copies ran while one was open for 8% of the time, Pallas kernels for 0%

commit v1 on v0

v1 whole, which is shorter than its diff:
```python
import jax
import jax.numpy as jnp
from jax import lax
from jax.sharding import Mesh, PartitionSpec as P

WEIGHTS = (-49.0 / 18.0, 1.5, -0.15, 1.0 / 90.0)
CENTRE = 6.05
HALFWIDTH = 4.05
SIZES = (("y", 4), ("xh", 2), ("core", 2), ("xl", 2), ("z1", 4), ("z0", 4))
BAND = ("y", "xh", "core")
PENCIL = ("xl", "z1", "z0")
NEAR = ("xl", "z0")
BF16 = jnp.bfloat16
F32 = jnp.float32


def halos(shard):
    size = lax.axis_size(PENCIL)
    up = [(i, (i + 1) % size) for i in range(size)]
    down = [(j, i) for i, j in up]
    return lax.ppermute(shard, PENCIL, up), lax.ppermute(shard, PENCIL, down)


def hamiltonian(field_low, before, after, potential):
    extended = jnp.concatenate([before, field_low, after], axis=1)
    field = field_low.astype(F32)
    planes = field.shape[1]
    total = 3.0 * WEIGHTS[0] * field
    for dist in range(1, 4):
        upper = extended[:, 3 + dist : 3 + dist + planes].astype(F32)
        lower = extended[:, 3 - dist : 3 - dist + planes].astype(F32)
        total = total + WEIGHTS[dist] * (upper + lower)
        for axis in (2, 3):
            ahead = jnp.roll(field_low, dist, axis).astype(F32)
            behind = jnp.roll(field_low, -dist, axis).astype(F32)
            total = total + WEIGHTS[dist] * (ahead + behind)
    return (field, -0.5 * total + potential[None] * field)


def gather_bands(rows):
    y, xh, core = (lax.axis_index(a) for a in BAND)
    ny = lax.axis_size("y")
    same = lax.all_gather(rows, "y", axis=0, tiled=True)
    others = []
    for dy in range(ny):
        pairs = [(a * 2 + b, ((a + dy) % ny) * 2 + 1 - b) for a in range(ny) for b in range(2)]
        others.append(lax.ppermute(rows, ("y", "xh"), pairs))
    mine = jnp.concatenate([same] + others, axis=0)
    theirs = lax.ppermute(mine, "core", [(0, 1), (1, 0)])
    step = jnp.arange(ny)
    ids = jnp.concatenate([(step * 2 + xh) * 2, (((y - step) % ny) * 2 + 1 - xh) * 2])
    return mine, theirs, jnp.concatenate([ids + core, ids + 1 - core])


def body(panels, potential, plan):
    orbitals = panels.shape[0]
    local_rows = panels.reshape(orbitals, -1)
    scale = 1.0 / (local_rows.shape[1] * lax.axis_size(PENCIL))
    before, after = halos(panels)
    mine, theirs, ids = gather_bands(local_rows)
    start, applied = hamiltonian(panels, before, after, potential)
    first = ((applied - CENTRE * start) / HALFWIDTH).astype(BF16)
    before, after = halos(first)
    firstf, applied_two = hamiltonian(first, before, after, potential)
    filtered = (2.0 * (applied_two - CENTRE * firstf) / HALFWIDTH - start).astype(BF16)
    local_filtered = filtered.reshape(orbitals, -1)
    gathered = jnp.concatenate([mine, theirs], axis=0)
    partial = lax.dot_general(
        local_filtered, gathered, (((1,), (1,)), ((), ())), preferred_element_type=F32
    )
    band = sum(lax.axis_index(a) * s for a, s in zip(BAND, (4, 2, 1)))
    earlier = jnp.repeat(plan[ids] < plan[band], orbitals, total_repeat_length=gathered.shape[0])
    near = lax.axis_size(NEAR)
    pieces = partial.astype(BF16).reshape(near, orbitals // near, -1)
    pieces = lax.all_to_all(pieces, NEAR, 0, 0)
    share = jnp.sum(pieces.astype(F32), axis=0).astype(BF16)
    far = lax.axis_size("z1")
    shares = lax.all_to_all(jnp.broadcast_to(share[None], (far,) + share.shape), "z1", 0, 0)
    summed = jnp.sum(shares.astype(F32), axis=0)
    part = jnp.where(earlier[None, :], summed * scale, 0.0).astype(BF16)
    coef = lax.all_to_all(jnp.broadcast_to(part[None], (near,) + part.shape), NEAR, 0, 0)
    coef = coef.reshape(orbitals, -1)
    removed = lax.dot_general(coef, gathered, (((1,), (0,)), ((), ())), preferred_element_type=F32)
    result = (local_filtered.astype(F32) - removed).astype(BF16)
    return result.reshape(panels.shape)


def solution(mesh):
    fine = Mesh(mesh.devices.reshape([s for _, s in SIZES]), [n for n, _ in SIZES])
    in_specs = (P(BAND, PENCIL, None, None), P(PENCIL, None, None), P())
    out_specs = P(BAND, PENCIL, None, None)
    return jax.shard_map(body, mesh=fine, in_specs=in_specs, out_specs=out_specs, check_vma=False)
```

time: 365 us -> 152 us (0.42)
  waiting for transfers between devices: 287 us -> 10 us
  starting transfers between devices: 20.3 us -> 55.2 us
  local copies, waits for them, and re-layouts: 14.4 us -> 32.2 us
  blocking collectives: 0 us -> 11.1 us
    psum x1 -> x0, waiting for transfers between devices: 249 us -> none  [body(): lax.psum(partial_sums.astype(jnp.bfloat16), 'pencil').astype(jnp.float32)]
    all_gather x1, waiting for transfers between devices: 28.3 us -> 0.01 us  [gather_bands(): same = lax.all_gather(rows, 'y', axis=0, tiled=True)]
    ppermute x4 -> x9, starting transfers between devices: 20.3 us -> 40.6 us  [the longest x4 21 us: halos(): return (lax.ppermute(shard, PENCIL, up), lax.ppermute(shard, PENCIL, down))]
    all_to_all x0 -> x2, starting transfers between devices: none -> 14.6 us  [the longest x1 11.2 us: body(): lax.all_to_all(jnp.broadcast_to(share[None], (far,) + share.shape), 'z1',...]
    all_to_all x0 -> x1, blocking collectives: none -> 11.1 us  [body(): lax.all_to_all(jnp.broadcast_to(part[None], (near,) + part.shape), NEAR,...]
    all_to_all x0 -> x2, waiting for transfers between devices: none -> 10 us  [the longest x1 7.24 us: body(): lax.all_to_all(jnp.broadcast_to(share[None], (far,) + share.shape), 'z1',...]
    ppermute x4 -> x9, waiting for transfers between devices: 9.9 us -> 0.02 us  [the longest x4 0.01 us: gather_bands(): others.append(lax.ppermute(rows, ('y', 'xh'), pairs))]
    unnamed x12 -> x26, local copies, waits for them, and re-layouts: 2.88 us -> 11.1 us
  transfers between devices with their start and end apart: 6 -> 12, of which waited for: 4 -> 2; matrix products, arithmetic and copies ran while one was open for 8% -> 31% of each run, Pallas kernels for 0% -> 0%
where the time goes in v1:
time: 152 us; the launch traced here: 151 us
  starting transfers between devices  55.2 us (36%)
  local copies, waits for them, and re-layouts  32.2 us (21%)
  other arithmetic  22.4 us (15%)
  between operations  13.9 us (9%)
  blocking collectives  11.1 us (7%)
  waiting for transfers between devices  10 us (7%)
  matrix products  6.68 us (4%)
    ppermute x4, starting transfers between devices, halos(): return (lax.ppermute(shard, PENCIL, up), lax.ppermute(shard, PENCIL, down))  21 us
    ppermute x4, starting transfers between devices, gather_bands(): others.append(lax.ppermute(rows, ('y', 'xh'), pairs))  17.5 us
    slice x24, local copies, waits for them, and re-layouts, hamiltonian(): behind = jnp.roll(field_low, -dist, axis).astype(F32)  17.2 us
    all_to_all x1, starting transfers between devices, body(): lax.all_to_all(jnp.broadcast_to(share[None], (far,) + share.shape), 'z1',...  11.2 us
    all_to_all x1, blocking collectives, body(): lax.all_to_all(jnp.broadcast_to(part[None], (near,) + part.shape), NEAR,...  11.1 us
    unnamed x26, local copies, waits for them, and re-layouts  11.1 us
    all_to_all x1, waiting for transfers between devices, body(): lax.all_to_all(jnp.broadcast_to(share[None], (far,) + share.shape), 'z1',...  7.24 us
    select_n x1, other arithmetic, body(): jnp.repeat(plan[ids] < plan[band], orbitals, total_repeat_length=gathered...  5.77 us
  transfers between devices with their start and end apart: 12, of which 2 were waited for; matrix products, arithmetic and copies ran while one was open for 31% of the time, Pallas kernels for 0%

profile of v1, /device:TPU:24, one launch (start us, length us, event | category | flops | bytes accessed | tf_op | source)
XLA Modules:
  0.0 151.4 jit_solution(4921052645119265777)
XLA Ops:
  6.5 1.9 %copy.13 = bf16[8,8,24,128]{3,1,2,0:T(8,128)(2,1)} copy(bf16[8,8,24,128]{3,2,1,0:T(8,128)(2,1)} %bitcast.55) | data formatting | bytes 786432
  8.4 4.9 %collective-permute-start.4 = (bf16[64,3072]{1,0:T(8,128)(2,1)}, bf16[64,3072]{1,0:T(8,128)(2,1)}, u32[]{:S(2)}, u32[]{:S(2)}) collective-permute-start(bf16[64,3072]{1,0:T(8,128)(2,1)} %bitcast.54), channel_id=1, source_target_pairs={{0,64},{64,0},{128,192},{192,128},{256,320},{320,256},{384,448},{4... | collective-permute-start | bytes 1179656 | tf_op jit(solution)/shard_map/ppermute | solution.py:47
  13.4 7.4 %collective-permute-start.5 = (bf16[64,3072]{1,0:T(8,128)(2,1)}, bf16[64,3072]{1,0:T(8,128)(2,1)}, u32[]{:S(2)}, u32[]{:S(2)}) collective-permute-start(bf16[64,3072]{1,0:T(8,128)(2,1)} %bitcast.54), channel_id=1, source_target_pairs={{0,192},{64,128},{128,320},{192,256},{256,448},{320,384},{384,64},... | collective-permute-start | bytes 1179656 | tf_op jit(solution)/shard_map/ppermute | solution.py:47
  20.8 1.9 %collective-permute-start.6 = (bf16[64,3072]{1,0:T(8,128)(2,1)}, bf16[64,3072]{1,0:T(8,128)(2,1)}, u32[]{:S(2)}, u32[]{:S(2)}) collective-permute-start(bf16[64,3072]{1,0:T(8,128)(2,1)} %bitcast.54), channel_id=1, source_target_pairs={{0,320},{64,256},{128,448},{192,384},{256,64},{320,0},{384,192},{4... | collective-permute-start | bytes 1179656 | tf_op jit(solution)/shard_map/ppermute | solution.py:47
  22.8 3.5 %collective-permute-start.1 = (bf16[64,3,8,128]{3,2,1,0:T(8,128)(2,1)}, bf16[64,3,8,128]{3,2,1,0:T(8,128)(2,1)S(1)}, u32[]{:S(2)}, u32[]{:S(2)}) collective-permute-start(bf16[64,3,8,128]{3,2,1,0:T(8,128)(2,1)} %param.5), channel_id=1, source_target_pairs={{0,1},{1,2},{2,3},{3,4},{4,5},{5,6},{6,7},{7,8},{8,9},{9,10},{10,1... | collective-permute-start | bytes 1179656 | tf_op jit(solution)/shard_map/ppermute | solution.py:21
  26.3 9.5 %collective-permute-start = (bf16[64,3,8,128]{3,2,1,0:T(8,128)(2,1)}, bf16[64,3,8,128]{3,2,1,0:T(8,128)(2,1)S(1)}, u32[]{:S(2)}, u32[]{:S(2)}) collective-permute-start(bf16[64,3,8,128]{3,2,1,0:T(8,128)(2,1)} %param.5), channel_id=1, source_target_pairs={{1,0},{2,1},{3,2},{4,3},{5,4},{6,5},{7,6},{8,7},{9,8},{10,9},{11,1... | collective-permute-start | bytes 1179656 | tf_op jit(solution)/shard_map/ppermute | solution.py:21
  35.8 1.3 fusion.64
  37.1 2.0 %fusion.65 = (bf16[64,3,1,128]{3,2,1,0:T(2,128)(2,1)}, bf16[64,3,1,128]{3,2,1,0:T(2,128)(2,1)}) fusion(bf16[64,3,8,128]{3,2,1,0:T(8,128)(2,1)} %param.5), kind=kLoop, calls=%fused_computation.125 | loop fusion | bytes 196608 | tf_op jit(solution)/shard_map/jit(_roll_static)/slice | solution.py:35
  39.1 1.3 fusion.62
  40.4 2.0 %fusion.63 = (bf16[64,3,8,1]{3,2,1,0:T(8,128)(2,1)S(1)}, bf16[64,3,8,1]{3,2,1,0:T(8,128)(2,1)}) fusion(bf16[64,3,8,128]{3,2,1,0:T(8,128)(2,1)} %param.5), kind=kLoop, calls=%fused_computation.123 | loop fusion | bytes 12288 | tf_op jit(solution)/shard_map/jit(_roll_static)/slice | solution.py:35
  42.4 1.0 fusion.60
  43.4 0.8 fusion.61
  44.2 1.1 fusion.58
  45.3 1.1 fusion.59
  46.4 1.0 fusion.56
  47.6 0.9 fusion.57
  48.5 1.0 fusion.54
  49.5 1.1 fusion.55
  50.6 0.7 gather_fusion
  51.3 0.6 dynamic_slice.3
  51.9 0.6 broadcast_compare_fusion
  52.5 0.6 iota_multiply_fusion
  53.1 3.2 %collective-permute-start.7 = (bf16[64,3072]{1,0:T(8,128)(2,1)}, bf16[64,3072]{1,0:T(8,128)(2,1)}, u32[]{:S(2)}, u32[]{:S(2)}) collective-permute-start(bf16[64,3072]{1,0:T(8,128)(2,1)} %bitcast.54), channel_id=1, source_target_pairs={{0,448},{64,384},{128,64},{192,0},{256,192},{320,128},{384,320},{4... | collective-permute-start | bytes 1179656 | tf_op jit(solution)/shard_map/ppermute | solution.py:47
  56.6 5.8 %fusion.29 = bf16[64,3,8,128]{3,2,1,0:T(8,128)(2,1)S(1)} fusion(bf16[64,3,8,128]{3,2,1,0:T(8,128)(2,1)S(1)} %collective-permute-done.1, bf16[64,3,8,128]{3,2,1,0:T(8,128)(2,1)S(1)} %collective-permute-done, bf16[64,3,8,128]{3,2,1,0:T(8,128)(2,1)S(1)} %copy-done.1, bf16[64,6,8,128]{3,2,1,0:T(8,128)(2,1)S(1)} %get-tuple-element.78, ...), kind=kLoop, calls=%fused_computation.43 | loop fusion | flops 17694720 | bytes 7876608 | tf_op jit(solution)/shard_map/convert_element_type | solution.py:62
  62.3 1.9 %collective-permute-start.3 = (bf16[64,3,8,128]{3,2,1,0:T(8,128)(2,1)S(1)}, bf16[64,3,8,128]{3,2,1,0:T(8,128)(2,1)S(1)}, u32[]{:S(2)}, u32[]{:S(2)}) collective-permute-start(bf16[64,3,8,128]{3,2,1,0:T(8,128)(2,1)S(1)} %fusion.29), channel_id=1, source_target_pairs={{0,1},{1,2},{2,3},{3,4},{4,5},{5,6},{6,7},{7,8},{8,9},{9,10},{10,1... | collective-permute-start | bytes 1179656 | tf_op jit(solution)/shard_map/ppermute | solution.py:21
  64.3 0.9 fusion.45
  65.2 1.6 %constant_dynamic-update-slice_fusion.8 = (bf16[512,3072]{1,0:T(8,128)(2,1)S(1)}, bf16[1024,3072]{1,0:T(8,128)(2,1)S(1)}) fusion(bf16[256,3072]{1,0:T(8,128)(2,1)} %all-gather.2.cloned.1.call-done), kind=kLoop, calls=%fused_computation.63 | loop fusion | bytes 4718592
  66.8 6.0 %collective-permute-start.2 = (bf16[64,3,8,128]{3,2,1,0:T(8,128)(2,1)S(1)}, bf16[64,3,8,128]{3,2,1,0:T(8,128)(2,1)S(1)}, u32[]{:S(2)}, u32[]{:S(2)}) collective-permute-start(bf16[64,3,8,128]{3,2,1,0:T(8,128)(2,1)S(1)} %fusion.29), channel_id=1, source_target_pairs={{1,0},{2,1},{3,2},{4,3},{5,4},{6,5},{7,6},{8,7},{9,8},{10,9},{11,1... | collective-permute-start | bytes 1179656 | tf_op jit(solution)/shard_map/ppermute | solution.py:21
  72.8 1.1 constant_dynamic-update-slice_fusion.7
  73.9 1.1 constant_dynamic-update-slice_fusion.6
  75.0 1.1 constant_dynamic-update-slice_fusion.5
  76.0 1.1 constant_dynamic-update-slice_fusion.4
  77.1 2.1 %collective-permute-start.8 = (bf16[512,3072]{1,0:T(8,128)(2,1)S(1)}, bf16[512,3072]{1,0:T(8,128)(2,1)S(1)}, u32[]{:S(2)}, u32[]{:S(2)}) collective-permute-start(bf16[512,3072]{1,0:T(8,128)(2,1)S(1)} %get-tuple-element.79), channel_id=1, source_target_pairs={{0,32},{32,0},{1,33},{33,1},{2,34},{34,2},{3,35},{35,3},{4,36},{36... | collective-permute-start | bytes 9437192 | tf_op jit(solution)/shard_map/ppermute | solution.py:49
  81.1 0.7 copy-done.5
  81.9 4.9 %fusion.30 = bf16[64,3,8,128]{3,2,1,0:T(8,128)(2,1)S(1)} fusion(bf16[64,3,8,128]{3,2,1,0:T(8,128)(2,1)S(1)} %copy-done.1, bf16[64,3,8,128]{3,2,1,0:T(8,128)(2,1)} %copy-done.5, bf16[64,3,8,128]{3,2,1,0:T(8,128)(2,1)S(1)} %collective-permute-done.2, bf16[64,3,8,128]{3,2,1,0:T(8,128)(2,1)S(1)} %fusion.29, bf16[64,3,7,128]{3,2,1,0:T(8,128)(2,1)S(1)} %get-tuple-element.50, ...), kind=kLoop, calls=%fused_computation.44 | loop fusion | flops 20447232 | bytes 6696960 | tf_op jit(solution)/shard_map/convert_element_type | solution.py:65
  87.0 2.7 %copy-done.2 = bf16[1024,3072]{1,0:T(8,128)(2,1)} copy-done((bf16[1024,3072]{1,0:T(8,128)(2,1)}, bf16[1024,3072]{1,0:T(8,128)(2,1)S(1)}, u32[]{:S(2)}) %copy-start.2) | copy-done | bytes 6291480
  89.6 2.7 %fusion.2 = bf16[8,8,1024]{2,1,0:T(8,128)(2,1)} fusion(bf16[1024,3072]{1,0:T(8,128)(2,1)S(1)} %constant_dynamic-update-slice_fusion.9, bf16[8,8,24,128]{3,2,1,0:T(8,128)(2,1)S(1)} %bitcast.56), kind=kOutput, calls=%fused_computation.12 | convolution fusion | flops 402718720 | bytes 6815744 | tf_op jit(solution)/shard_map/dot_general | solution.py:68
  92.3 3.4 %all-to-all-start = ((bf16[8,8,1024]{2,1,0:T(8,128)(2,1)}), bf16[8,8,1024]{2,1,0:T(8,128)(2,1)S(1)}, u32[]{:S(2)}, u32[]{:S(2)}) async-start(bf16[8,8,1024]{2,1,0:T(8,128)(2,1)} %fusion.2), calls=%async_computation | async-start | bytes 262144 | tf_op jit(solution)/shard_map/all_to_all | solution.py:75
  95.7 0.7 fusion.66
  96.5 4.5 %select_reduce_fusion = (pred[1024]{0:T(1024)(128)(4,1)S(1)}, pred[1024]{0:T(1024)(128)(4,1)S(1)}, pred[1024]{0:T(1024)(128)(4,1)S(1)}, pred[1024]{0:T(1024)(128...) fusion(pred[]{:T(512)} %bitcast.17, ...), kind=kLoop, calls=%fused_computation.71 | loop fusion | flops 23552 | bytes 18439 | tf_op jit(solution)/shard_map/jit(_take)/gather | solution.py:72
  101.0 2.8 %all-to-all-done = bf16[8,8,1024]{2,1,0:T(8,128)(2,1)S(1)} async-done(((bf16[8,8,1024]{2,1,0:T(8,128)(2,1)}), bf16[8,8,1024]{2,1,0:T(8,128)(2,1)S(1)}, u32[]{:S(2)}, u32[]{:S(2)}) %all-to-all-start) | async-done | bytes 131104 | tf_op jit(solution)/shard_map/all_to_all | solution.py:75
  103.8 0.6 broadcast_in_dim.44
  104.4 11.2 %all-to-all-start.1 = ((bf16[4,8,1024]{2,1,0:T(8,128)(2,1)}), bf16[4,8,1024]{2,1,0:T(8,128)(2,1)S(1)}, u32[]{:S(2)}, u32[]{:S(2)}) async-start(bf16[4,8,1024]{2,1,0:T(8,128)(2,1)} %broadcast_in_dim.44), calls=%async_computation.1 | async-start | bytes 131072 | tf_op jit(solution)/shard_map/all_to_all | solution.py:78
  115.6 5.8 %select_select_fusion = pred[1024]{0:T(1024)(128)(4,1)S(1)} fusion(pred[1024]{0:T(1024)(128)(4,1)S(1)} %get-tuple-element.26, pred[1024]{0:T(1024)(128)(4,1)S(1)} %get-tuple-element.25, pred[1024]{0:T(1024)(128)(4,1)S(1)} %get-tuple-element.20, pred[1024]{0:T(1024)(128)(4,1)S(1)} %get-tuple-element.21, pred[1024]{0:T(1024)(128)(4,1)S(1)} %get-tuple-element.22, ...), kind=kLoop, calls=%fused_computation.85 | loop fusion | flops 18432 | bytes 15401 | tf_op jit(solution)/shard_map/jit(_take)/select_n | solution.py:72
  121.4 7.2 %all-to-all-done.1 = bf16[4,8,1024]{2,1,0:T(8,128)(2,1)S(1)} async-done(((bf16[4,8,1024]{2,1,0:T(8,128)(2,1)}), bf16[4,8,1024]{2,1,0:T(8,128)(2,1)S(1)}, u32[]{:S(2)}, u32[]{:S(2)}) %all-to-all-start.1) | async-done | bytes 65568 | tf_op jit(solution)/shard_map/all_to_all | solution.py:78
  128.7 11.1 %all_to_all.15 = bf16[8,8,1024]{2,1,0:T(8,128)(2,1)S(1)} all-to-all(bf16[8,8,1024]{2,1,0:T(8,128)(2,1)S(1)} %broadcast_in_dim.46), channel_id=1, replica_groups=mesh['y'=4,'xh'=2,'core'=2,'xl'=2,'z1'=4,'z0'=4] {'xl','z0'}, dimensions={0} | all-to-all | bytes 262144 | tf_op jit(solution)/shard_map/all_to_all | solution.py:81
  139.8 4.0 %fusion.1 = bf16[8,8,24,128]{3,1,2,0:T(8,128)(2,1)S(1)} fusion(bf16[1024,3072]{1,0:T(8,128)(2,1)} %copy-done.2, bf16[8,8,24,128]{3,2,1,0:T(8,128)(2,1)S(1)} %bitcast.57, bf16[8,8,1024]{2,1,0:T(8,128)(2,1)S(1)} %all_to_all.15), kind=kOutput, calls=%fused_computation.7 | convolution fusion | flops 403243008 | bytes 7208960 | tf_op jit(solution)/shard_map/dot_general | solution.py:83
  143.8 0.8 copy.6
  (52 shorter events, 2.6 us)
Async XLA Ops:
  6.5 35.9 %copy-start.1 = (bf16[64,3,8,128]{3,2,1,0:T(8,128)(2,1)S(1)}, bf16[64,3,8,128]{3,2,1,0:T(8,128)(2,1)}, u32[]{:S(2)}) copy-start(bf16[64,3,8,128]{3,2,1,0:T(8,128)(2,1)} %param.5) | copy-start | bytes 1179652
  6.5 58.6 %all-gather.2.cloned.1.call-start = ((), (), s32[]{:S(2)}) async-start(), calls=%async_computation.3 | async-start | bytes 1966080 | tf_op jit(solution)/shard_map/all_gather | solution.py:43
  8.4 58.3 %collective-permute-start.4 = (bf16[64,3072]{1,0:T(8,128)(2,1)}, bf16[64,3072]{1,0:T(8,128)(2,1)}, u32[]{:S(2)}, u32[]{:S(2)}) collective-permute-start(bf16[64,3072]{1,0:T(8,128)(2,1)} %bitcast.54), channel_id=1, source_target_pairs={{0,64},{64,0},{128,192},{192,128},{256,320},{320,256},{384,448},{4... | collective-permute-start | bytes 1179656 | tf_op jit(solution)/shard_map/ppermute | solution.py:47
  13.4 60.5 %collective-permute-start.5 = (bf16[64,3072]{1,0:T(8,128)(2,1)}, bf16[64,3072]{1,0:T(8,128)(2,1)}, u32[]{:S(2)}, u32[]{:S(2)}) collective-permute-start(bf16[64,3072]{1,0:T(8,128)(2,1)} %bitcast.54), channel_id=1, source_target_pairs={{0,192},{64,128},{128,320},{192,256},{256,448},{320,384},{384,64},... | collective-permute-start | bytes 1179656 | tf_op jit(solution)/shard_map/ppermute | solution.py:47
  20.8 54.1 %collective-permute-start.6 = (bf16[64,3072]{1,0:T(8,128)(2,1)}, bf16[64,3072]{1,0:T(8,128)(2,1)}, u32[]{:S(2)}, u32[]{:S(2)}) collective-permute-start(bf16[64,3072]{1,0:T(8,128)(2,1)} %bitcast.54), channel_id=1, source_target_pairs={{0,320},{64,256},{128,448},{192,384},{256,64},{320,0},{384,192},{4... | collective-permute-start | bytes 1179656 | tf_op jit(solution)/shard_map/ppermute | solution.py:47
  22.8 30.3 %collective-permute-start.1 = (bf16[64,3,8,128]{3,2,1,0:T(8,128)(2,1)}, bf16[64,3,8,128]{3,2,1,0:T(8,128)(2,1)S(1)}, u32[]{:S(2)}, u32[]{:S(2)}) collective-permute-start(bf16[64,3,8,128]{3,2,1,0:T(8,128)(2,1)} %param.5), channel_id=1, source_target_pairs={{0,1},{1,2},{2,3},{3,4},{4,5},{5,6},{6,7},{7,8},{8,9},{9,10},{10,1... | collective-permute-start | bytes 1179656 | tf_op jit(solution)/shard_map/ppermute | solution.py:21
  26.3 30.2 %collective-permute-start = (bf16[64,3,8,128]{3,2,1,0:T(8,128)(2,1)}, bf16[64,3,8,128]{3,2,1,0:T(8,128)(2,1)S(1)}, u32[]{:S(2)}, u32[]{:S(2)}) collective-permute-start(bf16[64,3,8,128]{3,2,1,0:T(8,128)(2,1)} %param.5), channel_id=1, source_target_pairs={{1,0},{2,1},{3,2},{4,3},{5,4},{6,5},{7,6},{8,7},{9,8},{10,9},{11,1... | collective-permute-start | bytes 1179656 | tf_op jit(solution)/shard_map/ppermute | solution.py:21
  40.4 10.2 %copy-start = (s32[16]{0:T(128)S(1)}, s32[16]{0:T(128)}, u32[]{:S(2)}) copy-start(s32[16]{0:T(128)} %param.7) | copy-start | bytes 196
  43.4 13.2 %copy-start.6 = (f32[3,8,128]{2,1,0:T(8,128)S(1)}, f32[3,8,128]{2,1,0:T(8,128)}, u32[]{:S(2)}) copy-start(f32[3,8,128]{2,1,0:T(8,128)} %param.6) | copy-start | bytes 36868
  53.1 22.9 %collective-permute-start.7 = (bf16[64,3072]{1,0:T(8,128)(2,1)}, bf16[64,3072]{1,0:T(8,128)(2,1)}, u32[]{:S(2)}, u32[]{:S(2)}) collective-permute-start(bf16[64,3072]{1,0:T(8,128)(2,1)} %bitcast.54), channel_id=1, source_target_pairs={{0,448},{64,384},{128,64},{192,0},{256,192},{320,128},{384,320},{4... | collective-permute-start | bytes 1179656 | tf_op jit(solution)/shard_map/ppermute | solution.py:47
  62.3 18.7 %collective-permute-start.3 = (bf16[64,3,8,128]{3,2,1,0:T(8,128)(2,1)S(1)}, bf16[64,3,8,128]{3,2,1,0:T(8,128)(2,1)S(1)}, u32[]{:S(2)}, u32[]{:S(2)}) collective-permute-start(bf16[64,3,8,128]{3,2,1,0:T(8,128)(2,1)S(1)} %fusion.29), channel_id=1, source_target_pairs={{0,1},{1,2},{2,3},{3,4},{4,5},{5,6},{6,7},{7,8},{8,9},{9,10},{10,1... | collective-permute-start | bytes 1179656 | tf_op jit(solution)/shard_map/ppermute | solution.py:21
  66.8 14.3 %collective-permute-start.2 = (bf16[64,3,8,128]{3,2,1,0:T(8,128)(2,1)S(1)}, bf16[64,3,8,128]{3,2,1,0:T(8,128)(2,1)S(1)}, u32[]{:S(2)}, u32[]{:S(2)}) collective-permute-start(bf16[64,3,8,128]{3,2,1,0:T(8,128)(2,1)S(1)} %fusion.29), channel_id=1, source_target_pairs={{1,0},{2,1},{3,2},{4,3},{5,4},{6,5},{7,6},{8,7},{9,8},{10,9},{11,1... | collective-permute-start | bytes 1179656 | tf_op jit(solution)/shard_map/ppermute | solution.py:21
  77.1 9.6 %collective-permute-start.8 = (bf16[512,3072]{1,0:T(8,128)(2,1)S(1)}, bf16[512,3072]{1,0:T(8,128)(2,1)S(1)}, u32[]{:S(2)}, u32[]{:S(2)}) collective-permute-start(bf16[512,3072]{1,0:T(8,128)(2,1)S(1)} %get-tuple-element.79), channel_id=1, source_target_pairs={{0,32},{32,0},{1,33},{33,1},{2,34},{34,2},{3,35},{35,3},{4,36},{36... | collective-permute-start | bytes 9437192 | tf_op jit(solution)/shard_map/ppermute | solution.py:49
  79.5 2.3 %copy-start.3 = (bf16[64,3,3,128]{3,2,1,0:T(4,128)(2,1)S(1)}, bf16[64,3,3,128]{3,2,1,0:T(4,128)(2,1)}, u32[]{:S(2)}) copy-start(bf16[64,3,3,128]{3,2,1,0:T(4,128)(2,1)} %get-tuple-element.35) | copy-start | bytes 442372
  79.5 2.3 %copy-start.4 = (bf16[64,3,3,128]{3,2,1,0:T(4,128)(2,1)S(1)}, bf16[64,3,3,128]{3,2,1,0:T(4,128)(2,1)}, u32[]{:S(2)}) copy-start(bf16[64,3,3,128]{3,2,1,0:T(4,128)(2,1)} %get-tuple-element.36) | copy-start | bytes 442372
  81.1 0.7 copy-start.5
  86.7 9.7 %copy-start.7 = (s32[8,128]{1,0:T(8,128)S(1)}, s32[8,128]{1,0:T(8,128)}, u32[]{:S(2)}) copy-start(s32[8,128]{1,0:T(8,128)} %constant.136.clone.1) | copy-start | bytes 12292
  86.8 9.7 %copy-start.8 = (s32[8]{0:T(128)S(1)}, s32[8]{0:T(128)}, u32[]{:S(2)}) copy-start(s32[8]{0:T(128)} %iota_multiply_fusion) | copy-start | bytes 100
  87.0 2.7 %copy-start.2 = (bf16[1024,3072]{1,0:T(8,128)(2,1)}, bf16[1024,3072]{1,0:T(8,128)(2,1)S(1)}, u32[]{:S(2)}) copy-start(bf16[1024,3072]{1,0:T(8,128)(2,1)S(1)} %constant_dynamic-update-slice_fusion.9) | copy-start | bytes 18874372
  92.3 11.4 %all-to-all-start = ((bf16[8,8,1024]{2,1,0:T(8,128)(2,1)}), bf16[8,8,1024]{2,1,0:T(8,128)(2,1)S(1)}, u32[]{:S(2)}, u32[]{:S(2)}) async-start(bf16[8,8,1024]{2,1,0:T(8,128)(2,1)} %fusion.2), calls=%async_computation | async-start | bytes 262144 | tf_op jit(solution)/shard_map/all_to_all | solution.py:75
  104.4 24.2 %all-to-all-start.1 = ((bf16[4,8,1024]{2,1,0:T(8,128)(2,1)}), bf16[4,8,1024]{2,1,0:T(8,128)(2,1)S(1)}, u32[]{:S(2)}, u32[]{:S(2)}) async-start(bf16[4,8,1024]{2,1,0:T(8,128)(2,1)} %broadcast_in_dim.44), calls=%async_computation.1 | async-start | bytes 131072 | tf_op jit(solution)/shard_map/all_to_all | solution.py:78
Sparse Core Ops, SparseCore 0:
  9.5 44.2 all-gather.1

commit v2 on v1

v2 whole, which is shorter than its diff:
```python
import functools

import jax
import jax.numpy as jnp
from jax import lax
from jax.experimental import pallas as pl
from jax.experimental.pallas import tpu as pltpu
from jax.sharding import Mesh, PartitionSpec as P

WEIGHTS = (-49.0 / 18.0, 1.5, -0.15, 1.0 / 90.0)
CENTRE = 6.05
HALFWIDTH = 4.05
SIZES = (("y", 4), ("xh", 2), ("core", 2), ("xl", 2), ("z1", 4), ("z0", 4))
BAND = ("y", "xh", "core")
PENCIL = ("xl", "z1", "z0")
NEAR = ("xl", "z0")
BF16 = jnp.bfloat16
F32 = jnp.float32
LANES = 128
ROWS = 8
REACH = 3
VMEM = pl.BlockSpec(memory_space=pltpu.VMEM)
SMEM = pl.BlockSpec(memory_space=pltpu.SMEM)


def halos(shard):
    size = lax.axis_size(PENCIL)
    up = [(i, (i + 1) % size) for i in range(size)]
    down = [(j, i) for i, j in up]
    return lax.ppermute(shard, PENCIL, up), lax.ppermute(shard, PENCIL, down)


def stencil_kernel(second, before, mid, after, pot, *rest):
    if second:
        start, out, ext = rest
    else:
        out, ext = rest
    width = mid.shape[1]
    slices = width // LANES
    ext[:, :width] = before[...].astype(F32)
    ext[:, width : 2 * width] = mid[...].astype(F32)
    ext[:, 2 * width :] = after[...].astype(F32)
    factor = 2.0 if second else 1.0
    centre = (pot[...] - 1.5 * WEIGHTS[0] - CENTRE) * (factor / HALFWIDTH)

    def at(index):
        return ext[:, index * LANES : (index + 1) * LANES]

    for s in range(slices):
        plane, row = divmod(s, ROWS)
        own = at(slices + s)
        total = centre[s : s + 1, :] * own
        for dist in range(1, REACH + 1):
            near = at(slices + s + ROWS * dist) + at(slices + s - ROWS * dist)
            base = slices + plane * ROWS
            near = near + at(base + (row + dist) % ROWS) + at(base + (row - dist) % ROWS)
            near = near + pltpu.roll(own, dist, 1) + pltpu.roll(own, LANES - dist, 1)
            total = total + (-0.5 * factor * WEIGHTS[dist] / HALFWIDTH) * near
        cells = slice(s * LANES, (s + 1) * LANES)
        if second:
            total = total - start[:, cells].astype(F32)
        out[:, cells] = total.astype(BF16)


def stencil(before, mid, after, pot, start=None):
    args = [before, mid, after, pot] + ([] if start is None else [start])
    return pl.pallas_call(
        functools.partial(stencil_kernel, start is not None),
        out_shape=jax.ShapeDtypeStruct(mid.shape, BF16),
        in_specs=[VMEM] * len(args),
        out_specs=VMEM,
        scratch_shapes=[pltpu.VMEM((mid.shape[0], 3 * mid.shape[1]), F32)],
        compiler_params=pltpu.CompilerParams(vmem_limit_bytes=16 * 2**20),
        cost_estimate=pl.CostEstimate(flops=8_000_000, bytes_accessed=2_000_000, transcendentals=0),
        name="stencil_second" if start is not None else "stencil_first",
    )(*args)


def share_kernel(pieces, out):
    total = jnp.sum(pieces[...].astype(F32), axis=0).astype(BF16)
    for k in range(out.shape[0]):
        out[k] = total


def coef_kernel(scale, plan, place, pieces, out):
    total = jnp.sum(pieces[...].astype(F32), axis=0) * scale
    y, xh, core = place[0], place[1], place[2]
    turn = plan[4 * y + 2 * xh + core]
    bands = plan.shape[0]
    orbitals = total.shape[1] // bands
    low = lax.broadcasted_iota(jnp.int32, (total.shape[0], LANES), 1) < orbitals

    def earlier(block):
        group, source = divmod(block, bands // 4)
        side = xh if group < 2 else 1 - xh
        parity = core if group % 2 == 0 else 1 - core
        return (plan[4 * source + 2 * side + parity] < turn).astype(jnp.int32)

    for c in range(total.shape[1] // LANES):
        keep = jnp.where(low, earlier(2 * c), earlier(2 * c + 1)) > 0
        cells = slice(c * LANES, (c + 1) * LANES)
        part = jnp.where(keep, total[:, cells], 0.0).astype(BF16)
        for k in range(out.shape[0]):
            out[k, :, cells] = part


def along_y(block):
    count = lax.axis_size("y")
    wide = jnp.broadcast_to(block[None], (count,) + block.shape)
    return lax.all_to_all(wide, "y", 0, 0).reshape(count * block.shape[0], -1)


def swap_cores(block):
    return lax.ppermute(block, "core", [(0, 1), (1, 0)])


def body(panels, potential, plan):
    orbitals = panels.shape[0]
    rows = panels.reshape(orbitals, -1)
    pot = potential.reshape(-1, LANES)
    scale = 1.0 / (rows.shape[1] * lax.axis_size(PENCIL))
    near, far = lax.axis_size(NEAR), lax.axis_size("z1")
    before, after = halos(rows)
    swapped = lax.ppermute(rows, "xh", [(0, 1), (1, 0)])
    same = along_y(rows)
    swapped, before, after = lax.optimization_barrier((swapped, before, after))
    other = along_y(swapped)
    first = stencil(before, rows, after, pot)
    before, after = halos(first)
    same_core = swap_cores(same)
    other, before, after = lax.optimization_barrier((other, before, after))
    other_core = swap_cores(other)
    filtered = stencil(before, first, after, pot, rows)
    blocks = [same, same_core, other, other_core]

    def margins(other):
        return lax.dot_general(
            filtered, other, (((1,), (1,)), ((), ())), preferred_element_type=F32
        ).astype(BF16)

    partial = jnp.concatenate([margins(block) for block in blocks], axis=1)
    pieces = lax.all_to_all(partial.reshape(near, orbitals // near, -1), NEAR, 0, 0)
    share = (orbitals // near, partial.shape[1])
    shares = pl.pallas_call(
        share_kernel,
        out_shape=jax.ShapeDtypeStruct((far,) + share, BF16),
        in_specs=[VMEM],
        out_specs=VMEM,
        name="share",
    )(pieces)
    shares = lax.all_to_all(shares, "z1", 0, 0)
    place = jnp.stack([lax.axis_index(a) for a in BAND]).astype(jnp.int32)
    coef = pl.pallas_call(
        functools.partial(coef_kernel, scale),
        out_shape=jax.ShapeDtypeStruct((near,) + share, BF16),
        in_specs=[SMEM, SMEM, VMEM],
        out_specs=VMEM,
        name="coef",
    )(plan, place, shares)
    coef = lax.all_to_all(coef, NEAR, 0, 0).reshape(orbitals, -1)
    width = same.shape[0]
    removed = jnp.zeros(rows.shape, F32)
    for k, block in enumerate(blocks):
        removed = removed + lax.dot_general(
            coef[:, k * width : (k + 1) * width], block, (((1,), (0,)), ((), ())),
            preferred_element_type=F32,
        )
    result = (filtered.astype(F32) - removed).astype(BF16)
    return result.reshape(panels.shape)


def solution(mesh):
    fine = Mesh(mesh.devices.reshape([s for _, s in SIZES]), [n for n, _ in SIZES])
    in_specs = (P(BAND, PENCIL, None, None), P(PENCIL, None, None), P())
    out_specs = P(BAND, PENCIL, None, None)
    return jax.shard_map(body, mesh=fine, in_specs=in_specs, out_specs=out_specs, check_vma=False)
```

time: 152 us -> 127 us (0.84); the launches traced: 151 us -> 125 us
  waiting for transfers between devices: 10 us -> 39.7 us
  local copies, waits for them, and re-layouts: 32.2 us -> 5.69 us
  other arithmetic: 22.4 us -> 0.68 us
  between operations: 13.9 us -> 0.17 us
  starting transfers between devices: 55.2 us -> 42.1 us
  blocking collectives: 11.1 us -> 22 us
  Pallas kernels: 0 us -> 4.96 us
  matrix products: 6.68 us -> 9.63 us
    slice x24 -> x0, local copies, waits for them, and re-layouts: 17.2 us -> none  [hamiltonian(): behind = jnp.roll(field_low, -dist, axis).astype(F32)]
    ppermute x4, waiting for transfers between devices: 0.01 us -> 16.1 us  [halos(): return (lax.ppermute(shard, PENCIL, up), lax.ppermute(shard, PENCIL, down))]
    ppermute x5 -> x3, starting transfers between devices: 19.6 us -> 8.47 us  [the longest x1 4.64 us: body(): swapped = lax.ppermute(rows, 'xh', [(0, 1), (1, 0)])]
    all_to_all x1 -> x2, blocking collectives: 11.1 us -> 22 us  [the longest x1 11.2 us: body(): lax.all_to_all(partial.reshape(near, orbitals // near, -1), NEAR, 0, 0)]
    convert_element_type x3 -> x0, other arithmetic: 10.6 us -> none  [the longest x1 5.75 us: body(): first = ((applied - CENTRE * start) / HALFWIDTH).astype(BF16)]
    ppermute x5 -> x3, waiting for transfers between devices: 0.01 us -> 9.66 us  [the longest x1 9.65 us: body(): swapped = lax.ppermute(rows, 'xh', [(0, 1), (1, 0)])]
    unnamed x26 -> x8, local copies, waits for them, and re-layouts: 11.1 us -> 3.01 us
    select_n x2 -> x0, other arithmetic: 5.85 us -> none  [the longest x1 5.77 us: body(): jnp.repeat(plan[ids] < plan[band], orbitals, total_repeat_length=gathered...]
  transfers between devices with their start and end apart: 12 -> 10, of which waited for: 2 -> 7; matrix products, arithmetic and copies ran while one was open for 31% -> 4% of each run, Pallas kernels for 0% -> 1%
where the time goes in v2:
time: 127 us; the launch traced here: 125 us
  starting transfers between devices  42.1 us (33%)
  waiting for transfers between devices  39.7 us (31%)
  blocking collectives  22 us (17%)
  matrix products  9.63 us (8%)
  local copies, waits for them, and re-layouts  5.69 us (4%)
  Pallas kernels  4.96 us (4%)
    ppermute x4, waiting for transfers between devices, halos(): return (lax.ppermute(shard, PENCIL, up), lax.ppermute(shard, PENCIL, down))  16.1 us
    ppermute x4, starting transfers between devices, halos(): return (lax.ppermute(shard, PENCIL, up), lax.ppermute(shard, PENCIL, down))  15.6 us
    all_to_all x2, starting transfers between devices, along_y(): return lax.all_to_all(wide, 'y', 0, 0).reshape(count * block.shape[0], -1)  14.1 us
    all_to_all x1, waiting for transfers between devices, body(): shares = lax.all_to_all(shares, 'z1', 0, 0)  12.4 us
    all_to_all x1, blocking collectives, body(): lax.all_to_all(partial.reshape(near, orbitals // near, -1), NEAR, 0, 0)  11.2 us
    all_to_all x1, blocking collectives, body(): coef = lax.all_to_all(coef, NEAR, 0, 0).reshape(orbitals, -1)  10.8 us
    ppermute x1, waiting for transfers between devices, body(): swapped = lax.ppermute(rows, 'xh', [(0, 1), (1, 0)])  9.65 us
    dot_general x4, matrix products, margins(): lax.dot_general(filtered, other, (((1,), (1,)), ((), ())), preferred_elem...  5.22 us
  transfers between devices with their start and end apart: 10, of which 7 were waited for; matrix products, arithmetic and copies ran while one was open for 4% of the time, Pallas kernels for 1%

profile of v2, /device:TPU:24, one launch (start us, length us, event | category | flops | bytes accessed | tf_op | source)
XLA Modules:
  0.0 124.9 jit_solution(11515652473090682596)
XLA Ops:
  0.0 1.1 copy.7
  1.1 1.3 %broadcast_in_dim.5 = bf16[4,64,3072]{2,1,0:T(8,128)(2,1)} broadcast(bf16[64,3072]{1,0:T(8,128)(2,1)S(1)} %bitcast.30), dimensions={1,2} | broadcast | bytes 1966080 | tf_op jit(solution)/shard_map/broadcast_in_dim | solution.py:109
  2.4 9.1 %all-to-all-start.1 = ((bf16[4,64,3072]{2,1,0:T(8,128)(2,1)}), bf16[4,64,3072]{2,1,0:T(8,128)(2,1)S(1)}, u32[]{:S(2)}, u32[]{:S(2)}) async-start(bf16[4,64,3072]{2,1,0:T(8,128)(2,1)} %broadcast_in_dim.5), calls=%async_computation.1 | async-start | bytes 3145728 | tf_op jit(solution)/shard_map/all_to_all | solution.py:110
  11.5 7.9 %collective-permute-start.2 = (bf16[64,3072]{1,0:T(8,128)(2,1)S(1)}, bf16[64,3072]{1,0:T(8,128)(2,1)S(1)}, u32[]{:S(2)}, u32[]{:S(2)}) collective-permute-start(bf16[64,3072]{1,0:T(8,128)(2,1)S(1)} %bitcast.31), channel_id=1, source_target_pairs={{1,0},{2,1},{3,2},{4,3},{5,4},{6,5},{7,6},{8,7},{9,8},{10,9},{11,1... | collective-permute-start | bytes 1179656 | tf_op jit(solution)/shard_map/ppermute | solution.py:30
  19.4 1.9 %collective-permute-start.1 = (bf16[64,3072]{1,0:T(8,128)(2,1)S(1)}, bf16[64,3072]{1,0:T(8,128)(2,1)S(1)}, u32[]{:S(2)}, u32[]{:S(2)}) collective-permute-start(bf16[64,3072]{1,0:T(8,128)(2,1)S(1)} %bitcast.32), channel_id=1, source_target_pairs={{0,1},{1,2},{2,3},{3,4},{4,5},{5,6},{6,7},{7,8},{8,9},{9,10},{10,1... | collective-permute-start | bytes 1179656 | tf_op jit(solution)/shard_map/ppermute | solution.py:30
  21.3 4.6 %collective-permute-start = (bf16[64,3072]{1,0:T(8,128)(2,1)S(1)}, bf16[64,3072]{1,0:T(8,128)(2,1)S(1)}, u32[]{:S(2)}, u32[]{:S(2)}) collective-permute-start(bf16[64,3072]{1,0:T(8,128)(2,1)S(1)} %bitcast.33), channel_id=1, source_target_pairs={{0,64},{64,0},{1,65},{65,1},{2,66},{66,2},{3,67},{67,3},{4,68},{68... | collective-permute-start | bytes 1179656 | tf_op jit(solution)/shard_map/ppermute | solution.py:124
  26.0 1.2 collective-permute-done.2.after
  27.2 6.3 %collective-permute-done.1.before = bf16[64,3072]{1,0:T(8,128)(2,1)S(1)} collective-permute-done((bf16[64,3072]{1,0:T(8,128)(2,1)S(1)}, bf16[64,3072]{1,0:T(8,128)(2,1)S(1)}, u32[]{:S(2)}, u32[]{:S(2)}) %collective-permute-start.1) | collective-permute-done | bytes 393248 | tf_op jit(solution)/shard_map/ppermute | solution.py:30
  33.5 9.7 %collective-permute-done = bf16[64,3072]{1,0:T(8,128)(2,1)S(1)} collective-permute-done((bf16[64,3072]{1,0:T(8,128)(2,1)S(1)}, bf16[64,3072]{1,0:T(8,128)(2,1)S(1)}, u32[]{:S(2)}, u32[]{:S(2)}) %collective-permute-start) | collective-permute-done | bytes 393248 | tf_op jit(solution)/shard_map/ppermute | solution.py:124
  43.2 0.0 all-to-all-done.1
  43.2 1.3 %broadcast_in_dim.4 = bf16[4,64,3072]{2,1,0:T(8,128)(2,1)} broadcast(bf16[64,3072]{1,0:T(8,128)(2,1)S(1)} %collective-permute-done), dimensions={1,2} | broadcast | bytes 1966080 | tf_op jit(solution)/shard_map/broadcast_in_dim | solution.py:109
  44.5 0.0 copy-start
  44.5 4.9 %all-to-all-start = ((bf16[4,64,3072]{2,1,0:T(8,128)(2,1)}), bf16[4,64,3072]{2,1,0:T(8,128)(2,1)}, u32[]{:S(2)}, u32[]{:S(2)}) async-start(bf16[4,64,3072]{2,1,0:T(8,128)(2,1)} %broadcast_in_dim.4), calls=%async_computation | async-start | bytes 3145728 | tf_op jit(solution)/shard_map/all_to_all | solution.py:110
  49.4 0.0 copy-done
  49.5 0.9 stencil_first.1.mid
  50.3 1.9 %collective-permute-start.4 = (bf16[64,3072]{1,0:T(8,128)(2,1)S(1)}, bf16[64,3072]{1,0:T(8,128)(2,1)S(1)}, u32[]{:S(2)}, u32[]{:S(2)}) collective-permute-start(bf16[64,3072]{1,0:T(8,128)(2,1)S(1)} %stencil_first.1.mid), channel_id=1, source_target_pairs={{1,0},{2,1},{3,2},{4,3},{5,4},{6,5},{7,6},{8,7},{9,8},{10,9},{11,1... | collective-permute-start | bytes 1179656 | tf_op jit(solution)/shard_map/ppermute | solution.py:30
  52.3 3.9 %collective-permute-start.3 = (bf16[64,3072]{1,0:T(8,128)(2,1)S(1)}, bf16[64,3072]{1,0:T(8,128)(2,1)S(1)}, u32[]{:S(2)}, u32[]{:S(2)}) collective-permute-start(bf16[64,3072]{1,0:T(8,128)(2,1)S(1)} %stencil_first.1.mid), channel_id=1, source_target_pairs={{0,1},{1,2},{2,3},{3,4},{4,5},{5,6},{6,7},{7,8},{8,9},{9,10},{10,1... | collective-permute-start | bytes 1179656 | tf_op jit(solution)/shard_map/ppermute | solution.py:30
  56.2 1.9 %collective-permute-start.5 = (bf16[256,3072]{1,0:T(8,128)(2,1)S(1)}, bf16[256,3072]{1,0:T(8,128)(2,1)}, u32[]{:S(2)}, u32[]{:S(2)}) collective-permute-start(bf16[256,3072]{1,0:T(8,128)(2,1)S(1)} %bitcast.38), channel_id=1, source_target_pairs={{0,32},{32,0},{1,33},{33,1},{2,34},{34,2},{3,35},{35,3},{4,36},{36... | collective-permute-start | bytes 4718600 | tf_op jit(solution)/shard_map/ppermute | solution.py:114
  58.1 4.5 %collective-permute-done.4.after = bf16[64,3072]{1,0:T(8,128)(2,1)S(1)} collective-permute-done((bf16[64,3072]{1,0:T(8,128)(2,1)S(1)}, bf16[64,3072]{1,0:T(8,128)(2,1)S(1)}, u32[]{:S(2)}, u32[]{:S(2)}) %collective-permute-start.4) | collective-permute-done | bytes 393248 | tf_op jit(solution)/shard_map/ppermute | solution.py:30
  62.6 4.0 %collective-permute-done.3.before = bf16[64,3072]{1,0:T(8,128)(2,1)S(1)} collective-permute-done((bf16[64,3072]{1,0:T(8,128)(2,1)S(1)}, bf16[64,3072]{1,0:T(8,128)(2,1)S(1)}, u32[]{:S(2)}, u32[]{:S(2)}) %collective-permute-start.3) | collective-permute-done | bytes 393248 | tf_op jit(solution)/shard_map/ppermute | solution.py:30
  66.6 1.6 %all-to-all-done = bf16[4,64,3072]{2,1,0:T(8,128)(2,1)} async-done(((bf16[4,64,3072]{2,1,0:T(8,128)(2,1)}), bf16[4,64,3072]{2,1,0:T(8,128)(2,1)}, u32[]{:S(2)}, u32[]{:S(2)}) %all-to-all-start) | async-done | bytes 1572896 | tf_op jit(solution)/shard_map/all_to_all | solution.py:110
  68.3 1.9 %collective-permute-start.6 = (bf16[256,3072]{1,0:T(8,128)(2,1)}, bf16[256,3072]{1,0:T(8,128)(2,1)S(1)}, u32[]{:S(2)}, u32[]{:S(2)}) collective-permute-start(bf16[256,3072]{1,0:T(8,128)(2,1)} %bitcast), channel_id=1, source_target_pairs={{0,32},{32,0},{1,33},{33,1},{2,34},{34,2},{3,35},{35,3},{4,36},{36... | collective-permute-start | bytes 4718600 | tf_op jit(solution)/shard_map/ppermute | solution.py:114
  70.2 0.9 stencil_second.1
  71.1 2.0 %convolution_convert_fusion.1 = bf16[64,256]{1,0:T(8,128)(2,1)S(1)} fusion(bf16[64,3072]{1,0:T(8,128)(2,1)S(1)} %stencil_second.1, bf16[256,3072]{1,0:T(8,128)(2,1)} %bitcast), kind=kOutput, calls=%fused_computation.4 | convolution fusion | flops 100679680 | bytes 1998848 | tf_op jit(solution)/shard_map/dot_general | solution.py:137
  73.1 0.6 convolution_convert_fusion.3
  73.7 0.0 collective-permute-done.5
  73.7 2.0 %convolution_convert_fusion.2 = bf16[64,256]{1,0:T(8,128)(2,1)S(1)} fusion(bf16[64,3072]{1,0:T(8,128)(2,1)S(1)} %stencil_second.1, bf16[256,3072]{1,0:T(8,128)(2,1)} %collective-permute-done.5), kind=kOutput, calls=%fused_computation.5 | convolution fusion | flops 100679680 | bytes 1998848 | tf_op jit(solution)/shard_map/dot_general | solution.py:137
  75.7 0.0 collective-permute-done.6
  75.7 0.0 copy-start.1
  75.7 1.1 copy-done.1
  76.9 0.6 convolution_convert_fusion
  77.5 11.2 %all_to_all.25.pieces = bf16[8,8,1024]{2,1,0:T(8,128)(2,1)} all-to-all(bf16[8,8,1024]{2,1,0:T(8,128)(2,1)S(1)} %maximum_bitcast_fusion), channel_id=1, replica_groups=mesh['y'=4,'xh'=2,'core'=2,'xl'=2,'z1'=4,'z0'=4] {'xl','z0'}, dimensions={0} | all-to-all | bytes 262144 | tf_op jit(solution)/shard_map/all_to_all | solution.py:142
  88.7 0.0 copy-start.2
  88.7 1.7 %share.1 = bf16[4,8,1024]{2,1,0:T(8,128)(2,1)} custom-call(bf16[8,8,1024]{2,1,0:T(8,128)(2,1)} %all_to_all.25.pieces), custom_call_target="tpu_custom_call" | custom-call | tf_op jit(solution)/shard_map/share/pallas_call | solution.py:144
  90.3 3.9 %all-to-all-start.3 = ((bf16[4,8,1024]{2,1,0:T(8,128)(2,1)}), bf16[4,8,1024]{2,1,0:T(8,128)(2,1)}, u32[]{:S(2)}, u32[]{:S(2)}) async-start(bf16[4,8,1024]{2,1,0:T(8,128)(2,1)} %share.1), calls=%async_computation.3 | async-start | bytes 131072 | tf_op jit(solution)/shard_map/all_to_all | solution.py:151
  94.2 0.7 pad_add_fusion.place
  94.9 12.4 %all-to-all-done.3.pieces = bf16[4,8,1024]{2,1,0:T(8,128)(2,1)} async-done(((bf16[4,8,1024]{2,1,0:T(8,128)(2,1)}), bf16[4,8,1024]{2,1,0:T(8,128)(2,1)}, u32[]{:S(2)}, u32[]{:S(2)}) %all-to-all-start.3) | async-done | bytes 65568 | tf_op jit(solution)/shard_map/all_to_all | solution.py:151
  107.3 1.5 %coef.1 = bf16[8,8,1024]{2,1,0:T(8,128)(2,1)} custom-call(s32[16]{0:T(128)} %plan.1, s32[3]{0:T(128)} %pad_add_fusion.place, bf16[4,8,1024]{2,1,0:T(8,128)(2,1)} %all-to-all-done.3.pieces), custom_call_target="tpu_custom_call" | custom-call | tf_op jit(solution)/shard_map/coef/pallas_call | solution.py:153
  108.8 10.8 %all_to_all.26 = bf16[8,8,1024]{2,1,0:T(8,128)(2,1)S(1)} all-to-all(bf16[8,8,1024]{2,1,0:T(8,128)(2,1)} %coef.1), channel_id=1, replica_groups=mesh['y'=4,'xh'=2,'core'=2,'xl'=2,'z1'=4,'z0'=4] {'xl','z0'}, dimensions={0} | all-to-all | bytes 262144 | tf_op jit(solution)/shard_map/all_to_all | solution.py:160
  119.6 0.4 fusion.8
  120.0 0.0 copy-done.2
  120.0 0.4 fusion.2
  120.4 1.8 %convolution_add_fusion.1 = f32[64,3072]{1,0:T(8,128)S(1)} fusion(f32[64,3072]{1,0:T(8,128)S(1)} %fusion.8, bf16[256,3072]{1,0:T(8,128)(2,1)} %collective-permute-done.5, bf16[64,1024]{1,0:T(8,128)(2,1)S(1)} %bitcast.43), kind=kOutput, calls=%fused_computation.1 | convolution fusion | flops 100859904 | bytes 3178496 | tf_op jit(solution)/shard_map/dot_general | solution.py:164
  122.2 1.8 %fusion.1 = bf16[8,8,24,128]{3,1,2,0:T(8,128)(2,1)S(1)} fusion(bf16[64,3072]{1,0:T(8,128)(2,1)S(1)} %stencil_second.1, f32[64,3072]{1,0:T(8,128)S(1)} %fusion.2, f32[64,3072]{1,0:T(8,128)S(1)} %convolution_add_fusion.1, bf16[256,3072]{1,0:T(8,128)(2,1)} %bitcast, bf16[64,1024]{1,0:T(8,128)(2,1)S(1)} %bitcast.44), kind=kOutput, calls=%fused_computation.8 | convolution fusion | flops 101646336 | bytes 3964928 | tf_op jit(solution)/shard_map/dot_general | solution.py:164
  124.1 0.8 copy.5
  (1 shorter events, 0.0 us)
Async XLA Ops:
  2.4 40.8 %all-to-all-start.1 = ((bf16[4,64,3072]{2,1,0:T(8,128)(2,1)}), bf16[4,64,3072]{2,1,0:T(8,128)(2,1)S(1)}, u32[]{:S(2)}, u32[]{:S(2)}) async-start(bf16[4,64,3072]{2,1,0:T(8,128)(2,1)} %broadcast_in_dim.5), calls=%async_computation.1 | async-start | bytes 3145728 | tf_op jit(solution)/shard_map/all_to_all | solution.py:110
  11.5 15.7 %collective-permute-start.2 = (bf16[64,3072]{1,0:T(8,128)(2,1)S(1)}, bf16[64,3072]{1,0:T(8,128)(2,1)S(1)}, u32[]{:S(2)}, u32[]{:S(2)}) collective-permute-start(bf16[64,3072]{1,0:T(8,128)(2,1)S(1)} %bitcast.31), channel_id=1, source_target_pairs={{1,0},{2,1},{3,2},{4,3},{5,4},{6,5},{7,6},{8,7},{9,8},{10,9},{11,1... | collective-permute-start | bytes 1179656 | tf_op jit(solution)/shard_map/ppermute | solution.py:30
  19.4 14.1 %collective-permute-start.1 = (bf16[64,3072]{1,0:T(8,128)(2,1)S(1)}, bf16[64,3072]{1,0:T(8,128)(2,1)S(1)}, u32[]{:S(2)}, u32[]{:S(2)}) collective-permute-start(bf16[64,3072]{1,0:T(8,128)(2,1)S(1)} %bitcast.32), channel_id=1, source_target_pairs={{0,1},{1,2},{2,3},{3,4},{4,5},{5,6},{6,7},{7,8},{8,9},{9,10},{10,1... | collective-permute-start | bytes 1179656 | tf_op jit(solution)/shard_map/ppermute | solution.py:30
  21.3 21.8 %collective-permute-start = (bf16[64,3072]{1,0:T(8,128)(2,1)S(1)}, bf16[64,3072]{1,0:T(8,128)(2,1)S(1)}, u32[]{:S(2)}, u32[]{:S(2)}) collective-permute-start(bf16[64,3072]{1,0:T(8,128)(2,1)S(1)} %bitcast.33), channel_id=1, source_target_pairs={{0,64},{64,0},{1,65},{65,1},{2,66},{66,2},{3,67},{67,3},{4,68},{68... | collective-permute-start | bytes 1179656 | tf_op jit(solution)/shard_map/ppermute | solution.py:124
  44.5 4.9 %copy-start = (f32[3,8,128]{2,1,0:T(8,128)S(1)}, f32[3,8,128]{2,1,0:T(8,128)}, u32[]{:S(2)}) copy-start(f32[3,8,128]{2,1,0:T(8,128)} %param.4) | copy-start | bytes 36868
  44.5 23.7 %all-to-all-start = ((bf16[4,64,3072]{2,1,0:T(8,128)(2,1)}), bf16[4,64,3072]{2,1,0:T(8,128)(2,1)}, u32[]{:S(2)}, u32[]{:S(2)}) async-start(bf16[4,64,3072]{2,1,0:T(8,128)(2,1)} %broadcast_in_dim.4), calls=%async_computation | async-start | bytes 3145728 | tf_op jit(solution)/shard_map/all_to_all | solution.py:110
  50.3 12.3 %collective-permute-start.4 = (bf16[64,3072]{1,0:T(8,128)(2,1)S(1)}, bf16[64,3072]{1,0:T(8,128)(2,1)S(1)}, u32[]{:S(2)}, u32[]{:S(2)}) collective-permute-start(bf16[64,3072]{1,0:T(8,128)(2,1)S(1)} %stencil_first.1.mid), channel_id=1, source_target_pairs={{1,0},{2,1},{3,2},{4,3},{5,4},{6,5},{7,6},{8,7},{9,8},{10,9},{11,1... | collective-permute-start | bytes 1179656 | tf_op jit(solution)/shard_map/ppermute | solution.py:30
  52.3 14.4 %collective-permute-start.3 = (bf16[64,3072]{1,0:T(8,128)(2,1)S(1)}, bf16[64,3072]{1,0:T(8,128)(2,1)S(1)}, u32[]{:S(2)}, u32[]{:S(2)}) collective-permute-start(bf16[64,3072]{1,0:T(8,128)(2,1)S(1)} %stencil_first.1.mid), channel_id=1, source_target_pairs={{0,1},{1,2},{2,3},{3,4},{4,5},{5,6},{6,7},{7,8},{8,9},{9,10},{10,1... | collective-permute-start | bytes 1179656 | tf_op jit(solution)/shard_map/ppermute | solution.py:30
  56.2 17.5 %collective-permute-start.5 = (bf16[256,3072]{1,0:T(8,128)(2,1)S(1)}, bf16[256,3072]{1,0:T(8,128)(2,1)}, u32[]{:S(2)}, u32[]{:S(2)}) collective-permute-start(bf16[256,3072]{1,0:T(8,128)(2,1)S(1)} %bitcast.38), channel_id=1, source_target_pairs={{0,32},{32,0},{1,33},{33,1},{2,34},{34,2},{3,35},{35,3},{4,36},{36... | collective-permute-start | bytes 4718600 | tf_op jit(solution)/shard_map/ppermute | solution.py:114
  68.3 7.4 %collective-permute-start.6 = (bf16[256,3072]{1,0:T(8,128)(2,1)}, bf16[256,3072]{1,0:T(8,128)(2,1)S(1)}, u32[]{:S(2)}, u32[]{:S(2)}) collective-permute-start(bf16[256,3072]{1,0:T(8,128)(2,1)} %bitcast), channel_id=1, source_target_pairs={{0,32},{32,0},{1,33},{33,1},{2,34},{34,2},{3,35},{35,3},{4,36},{36... | collective-permute-start | bytes 4718600 | tf_op jit(solution)/shard_map/ppermute | solution.py:114
  75.7 1.2 copy-start.1
  88.7 31.4 %copy-start.2 = (bf16[256,3072]{1,0:T(8,128)(2,1)S(1)}, bf16[256,3072]{1,0:T(8,128)(2,1)}, u32[]{:S(2)}) copy-start(bf16[256,3072]{1,0:T(8,128)(2,1)} %copy-done.1) | copy-start | bytes 4718596
  90.3 17.0 %all-to-all-start.3 = ((bf16[4,8,1024]{2,1,0:T(8,128)(2,1)}), bf16[4,8,1024]{2,1,0:T(8,128)(2,1)}, u32[]{:S(2)}, u32[]{:S(2)}) async-start(bf16[4,8,1024]{2,1,0:T(8,128)(2,1)} %share.1), calls=%async_computation.3 | async-start | bytes 131072 | tf_op jit(solution)/shard_map/all_to_all | solution.py:151

commit v3 on v2

--- a/solution.py
+++ b/solution.py
@@ -21,6 +21,7 @@
 REACH = 3
 VMEM = pl.BlockSpec(memory_space=pltpu.VMEM)
 SMEM = pl.BlockSpec(memory_space=pltpu.SMEM)
+PARAMS = pltpu.CompilerParams(vmem_limit_bytes=16 * 2**20)
 
 
 def halos(shard):
@@ -70,7 +71,7 @@
         in_specs=[VMEM] * len(args),
         out_specs=VMEM,
         scratch_shapes=[pltpu.VMEM((mid.shape[0], 3 * mid.shape[1]), F32)],
-        compiler_params=pltpu.CompilerParams(vmem_limit_bytes=16 * 2**20),
+        compiler_params=PARAMS,
         cost_estimate=pl.CostEstimate(flops=8_000_000, bytes_accessed=2_000_000, transcendentals=0),
         name="stencil_second" if start is not None else "stencil_first",
     )(*args)
@@ -104,10 +105,12 @@
             out[k, :, cells] = part
 
 
-def along_y(block):
-    count = lax.axis_size("y")
-    wide = jnp.broadcast_to(block[None], (count,) + block.shape)
-    return lax.all_to_all(wide, "y", 0, 0).reshape(count * block.shape[0], -1)
+def widen(block):
+    return jnp.broadcast_to(block[None], (lax.axis_size("y"),) + block.shape)
+
+
+def along_y(wide):
+    return lax.all_to_all(wide, "y", 0, 0).reshape(-1, wide.shape[-1])
 
 
 def swap_cores(block):
@@ -122,9 +125,10 @@
     near, far = lax.axis_size(NEAR), lax.axis_size("z1")
     before, after = halos(rows)
     swapped = lax.ppermute(rows, "xh", [(0, 1), (1, 0)])
-    same = along_y(rows)
-    swapped, before, after = lax.optimization_barrier((swapped, before, after))
-    other = along_y(swapped)
+    same = along_y(widen(rows))
+    wide = widen(swapped)
+    before, after, wide = lax.optimization_barrier((before, after, wide))
+    other = along_y(wide)
     first = stencil(before, rows, after, pot)
     before, after = halos(first)
     same_core = swap_cores(same)
@@ -146,6 +150,7 @@
         out_shape=jax.ShapeDtypeStruct((far,) + share, BF16),
         in_specs=[VMEM],
         out_specs=VMEM,
+        compiler_params=PARAMS,
         name="share",
     )(pieces)
     shares = lax.all_to_all(shares, "z1", 0, 0)
@@ -155,6 +160,7 @@
         out_shape=jax.ShapeDtypeStruct((near,) + share, BF16),
         in_specs=[SMEM, SMEM, VMEM],
         out_specs=VMEM,
+        compiler_params=PARAMS,
         name="coef",
     )(plan, place, shares)
     coef = lax.all_to_all(coef, NEAR, 0, 0).reshape(orbitals, -1)

time: 127 us -> 117 us (0.921)
  waiting for transfers between devices: 39.7 us -> 33.8 us
  Pallas kernels: 4.96 us -> 2.98 us
  blocking collectives: 22 us -> 20.4 us
    ppermute x1, waiting for transfers between devices: 9.65 us -> 0.01 us  [body(): swapped = lax.ppermute(rows, 'xh', [(0, 1), (1, 0)])]
    ppermute x4, waiting for transfers between devices: 16.1 us -> 20.8 us  [halos(): return (lax.ppermute(shard, PENCIL, up), lax.ppermute(shard, PENCIL, down))]
    ppermute x1, starting transfers between devices: 4.64 us -> 1.91 us  [body(): swapped = lax.ppermute(rows, 'xh', [(0, 1), (1, 0)])]
    ppermute x4, starting transfers between devices: 15.6 us -> 18.2 us  [halos(): return (lax.ppermute(shard, PENCIL, up), lax.ppermute(shard, PENCIL, down))]
    all_to_all x2, waiting for transfers between devices: 1.62 us -> 0.01 us  [along_y(): return lax.all_to_all(wide, 'y', 0, 0).reshape(-1, wide.shape[-1])]
    unnamed x8 -> x10, local copies, waits for them, and re-layouts: 3.01 us -> 2.43 us
  transfers between devices with their start and end apart: 10 -> 10, of which waited for: 7 -> 5; matrix products, arithmetic and copies ran while one was open for 4% -> 5% of each run, Pallas kernels for 1% -> 2%
where the time goes in v3:
time: 117 us; the launch traced here: 115 us
  starting transfers between devices  42.8 us (37%)
  waiting for transfers between devices  33.8 us (29%)
  blocking collectives  20.4 us (17%)
  matrix products  9.64 us (8%)
  local copies, waits for them, and re-layouts  5.13 us (4%)
  Pallas kernels  2.98 us (3%)
    ppermute x4, waiting for transfers between devices, halos(): return (lax.ppermute(shard, PENCIL, up), lax.ppermute(shard, PENCIL, down))  20.8 us
    ppermute x4, starting transfers between devices, halos(): return (lax.ppermute(shard, PENCIL, up), lax.ppermute(shard, PENCIL, down))  18.2 us
    all_to_all x2, starting transfers between devices, along_y(): return lax.all_to_all(wide, 'y', 0, 0).reshape(-1, wide.shape[-1])  14.1 us
    all_to_all x1, waiting for transfers between devices, body(): shares = lax.all_to_all(shares, 'z1', 0, 0)  12.9 us
    all_to_all x1, blocking collectives, body(): lax.all_to_all(partial.reshape(near, orbitals // near, -1), NEAR, 0, 0)  10.5 us
    all_to_all x1, blocking collectives, body(): coef = lax.all_to_all(coef, NEAR, 0, 0).reshape(orbitals, -1)  9.91 us
    dot_general x4, matrix products, margins(): lax.dot_general(filtered, other, (((1,), (1,)), ((), ())), preferred_elem...  5.22 us
    all_to_all x1, starting transfers between devices, body(): shares = lax.all_to_all(shares, 'z1', 0, 0)  4.87 us
  transfers between devices with their start and end apart: 10, of which 5 were waited for; matrix products, arithmetic and copies ran while one was open for 5% of the time, Pallas kernels for 2%

profile of v3, /device:TPU:24, one launch (start us, length us, event | category | flops | bytes accessed | tf_op | source)
XLA Modules:
  0.0 115.0 jit_solution(14641252012263508887)
XLA Ops:
  0.0 1.1 copy.7
  1.1 1.4 %broadcast_in_dim.5 = bf16[4,64,3072]{2,1,0:T(8,128)(2,1)} broadcast(bf16[64,3072]{1,0:T(8,128)(2,1)S(1)} %bitcast.30), dimensions={1,2} | broadcast | bytes 1966080 | tf_op jit(solution)/shard_map/broadcast_in_dim | solution.py:109
  2.4 9.1 %all-to-all-start.1 = ((bf16[4,64,3072]{2,1,0:T(8,128)(2,1)}), bf16[4,64,3072]{2,1,0:T(8,128)(2,1)S(1)}, u32[]{:S(2)}, u32[]{:S(2)}) async-start(bf16[4,64,3072]{2,1,0:T(8,128)(2,1)} %broadcast_in_dim.5), calls=%async_computation.1 | async-start | bytes 3145728 | tf_op jit(solution)/shard_map/all_to_all | solution.py:113
  11.6 1.9 %collective-permute-start.2 = (bf16[64,3072]{1,0:T(8,128)(2,1)S(1)}, bf16[64,3072]{1,0:T(8,128)(2,1)S(1)}, u32[]{:S(2)}, u32[]{:S(2)}) collective-permute-start(bf16[64,3072]{1,0:T(8,128)(2,1)S(1)} %bitcast.31), channel_id=1, source_target_pairs={{0,64},{64,0},{1,65},{65,1},{2,66},{66,2},{3,67},{67,3},{4,68},{68... | collective-permute-start | bytes 1179656 | tf_op jit(solution)/shard_map/ppermute | solution.py:127
  13.5 10.0 %collective-permute-start.1 = (bf16[64,3072]{1,0:T(8,128)(2,1)S(1)}, bf16[64,3072]{1,0:T(8,128)(2,1)S(1)}, u32[]{:S(2)}, u32[]{:S(2)}) collective-permute-start(bf16[64,3072]{1,0:T(8,128)(2,1)S(1)} %bitcast.32), channel_id=1, source_target_pairs={{1,0},{2,1},{3,2},{4,3},{5,4},{6,5},{7,6},{8,7},{9,8},{10,9},{11,1... | collective-permute-start | bytes 1179656 | tf_op jit(solution)/shard_map/ppermute | solution.py:31
  23.5 1.9 %collective-permute-start = (bf16[64,3072]{1,0:T(8,128)(2,1)S(1)}, bf16[64,3072]{1,0:T(8,128)(2,1)S(1)}, u32[]{:S(2)}, u32[]{:S(2)}) collective-permute-start(bf16[64,3072]{1,0:T(8,128)(2,1)S(1)} %bitcast.33), channel_id=1, source_target_pairs={{0,1},{1,2},{2,3},{3,4},{4,5},{5,6},{6,7},{7,8},{8,9},{9,10},{10,1... | collective-permute-start | bytes 1179656 | tf_op jit(solution)/shard_map/ppermute | solution.py:31
  25.4 0.0 collective-permute-done.2
  25.4 5.6 %collective-permute-done.1.after = bf16[64,3072]{1,0:T(8,128)(2,1)S(1)} collective-permute-done((bf16[64,3072]{1,0:T(8,128)(2,1)S(1)}, bf16[64,3072]{1,0:T(8,128)(2,1)S(1)}, u32[]{:S(2)}, u32[]{:S(2)}) %collective-permute-start.1) | collective-permute-done | bytes 393248 | tf_op jit(solution)/shard_map/ppermute | solution.py:31
  31.0 6.2 %collective-permute-done.before = bf16[64,3072]{1,0:T(8,128)(2,1)S(1)} collective-permute-done((bf16[64,3072]{1,0:T(8,128)(2,1)S(1)}, bf16[64,3072]{1,0:T(8,128)(2,1)S(1)}, u32[]{:S(2)}, u32[]{:S(2)}) %collective-permute-start) | collective-permute-done | bytes 393248 | tf_op jit(solution)/shard_map/ppermute | solution.py:31
  37.2 1.3 %broadcast_in_dim.4 = bf16[4,64,3072]{2,1,0:T(8,128)(2,1)} broadcast(bf16[64,3072]{1,0:T(8,128)(2,1)S(1)} %collective-permute-done.2), dimensions={1,2} | broadcast | bytes 1966080 | tf_op jit(solution)/shard_map/broadcast_in_dim | solution.py:109
  38.5 0.0 copy-start
  38.6 0.0 all-to-all-done.1
  38.6 4.9 %all-to-all-start = ((bf16[4,64,3072]{2,1,0:T(8,128)(2,1)}), bf16[4,64,3072]{2,1,0:T(8,128)(2,1)}, u32[]{:S(2)}, u32[]{:S(2)}) async-start(bf16[4,64,3072]{2,1,0:T(8,128)(2,1)} %broadcast_in_dim.4), calls=%async_computation | async-start | bytes 3145728 | tf_op jit(solution)/shard_map/all_to_all | solution.py:113
  43.5 0.0 copy-done
  43.5 0.9 stencil_first.1.mid
  44.4 4.3 %collective-permute-start.4 = (bf16[64,3072]{1,0:T(8,128)(2,1)S(1)}, bf16[64,3072]{1,0:T(8,128)(2,1)S(1)}, u32[]{:S(2)}, u32[]{:S(2)}) collective-permute-start(bf16[64,3072]{1,0:T(8,128)(2,1)S(1)} %stencil_first.1.mid), channel_id=1, source_target_pairs={{1,0},{2,1},{3,2},{4,3},{5,4},{6,5},{7,6},{8,7},{9,8},{10,9},{11,1... | collective-permute-start | bytes 1179656 | tf_op jit(solution)/shard_map/ppermute | solution.py:31
  48.7 1.9 %collective-permute-start.3 = (bf16[64,3072]{1,0:T(8,128)(2,1)S(1)}, bf16[64,3072]{1,0:T(8,128)(2,1)S(1)}, u32[]{:S(2)}, u32[]{:S(2)}) collective-permute-start(bf16[64,3072]{1,0:T(8,128)(2,1)S(1)} %stencil_first.1.mid), channel_id=1, source_target_pairs={{0,1},{1,2},{2,3},{3,4},{4,5},{5,6},{6,7},{7,8},{8,9},{9,10},{10,1... | collective-permute-start | bytes 1179656 | tf_op jit(solution)/shard_map/ppermute | solution.py:31
  50.6 1.9 %collective-permute-start.5 = (bf16[256,3072]{1,0:T(8,128)(2,1)S(1)}, bf16[256,3072]{1,0:T(8,128)(2,1)}, u32[]{:S(2)}, u32[]{:S(2)}) collective-permute-start(bf16[256,3072]{1,0:T(8,128)(2,1)S(1)} %bitcast.38), channel_id=1, source_target_pairs={{0,32},{32,0},{1,33},{33,1},{2,34},{34,2},{3,35},{35,3},{4,36},{36... | collective-permute-start | bytes 4718600 | tf_op jit(solution)/shard_map/ppermute | solution.py:117
  52.6 2.8 %collective-permute-done.4.after = bf16[64,3072]{1,0:T(8,128)(2,1)S(1)} collective-permute-done((bf16[64,3072]{1,0:T(8,128)(2,1)S(1)}, bf16[64,3072]{1,0:T(8,128)(2,1)S(1)}, u32[]{:S(2)}, u32[]{:S(2)}) %collective-permute-start.4) | collective-permute-done | bytes 393248 | tf_op jit(solution)/shard_map/ppermute | solution.py:31
  55.4 6.2 %collective-permute-done.3.before = bf16[64,3072]{1,0:T(8,128)(2,1)S(1)} collective-permute-done((bf16[64,3072]{1,0:T(8,128)(2,1)S(1)}, bf16[64,3072]{1,0:T(8,128)(2,1)S(1)}, u32[]{:S(2)}, u32[]{:S(2)}) %collective-permute-start.3) | collective-permute-done | bytes 393248 | tf_op jit(solution)/shard_map/ppermute | solution.py:31
  61.6 0.0 all-to-all-done
  61.6 1.9 %collective-permute-start.6 = (bf16[256,3072]{1,0:T(8,128)(2,1)}, bf16[256,3072]{1,0:T(8,128)(2,1)S(1)}, u32[]{:S(2)}, u32[]{:S(2)}) collective-permute-start(bf16[256,3072]{1,0:T(8,128)(2,1)} %bitcast), channel_id=1, source_target_pairs={{0,32},{32,0},{1,33},{33,1},{2,34},{34,2},{3,35},{35,3},{4,36},{36... | collective-permute-start | bytes 4718600 | tf_op jit(solution)/shard_map/ppermute | solution.py:117
  63.5 0.9 stencil_second.1
  64.4 2.0 %convolution_convert_fusion.1 = bf16[64,256]{1,0:T(8,128)(2,1)S(1)} fusion(bf16[64,3072]{1,0:T(8,128)(2,1)S(1)} %stencil_second.1, bf16[256,3072]{1,0:T(8,128)(2,1)} %bitcast), kind=kOutput, calls=%fused_computation.4 | convolution fusion | flops 100679680 | bytes 1998848 | tf_op jit(solution)/shard_map/dot_general | solution.py:141
  66.4 0.6 convolution_convert_fusion.3
  67.0 0.0 collective-permute-done.5
  67.1 2.0 %convolution_convert_fusion.2 = bf16[64,256]{1,0:T(8,128)(2,1)S(1)} fusion(bf16[64,3072]{1,0:T(8,128)(2,1)S(1)} %stencil_second.1, bf16[256,3072]{1,0:T(8,128)(2,1)} %collective-permute-done.5), kind=kOutput, calls=%fused_computation.5 | convolution fusion | flops 100679680 | bytes 1998848 | tf_op jit(solution)/shard_map/dot_general | solution.py:141
  69.1 0.0 copy-start.1
  69.1 0.0 collective-permute-done.6
  69.1 0.0 copy-start.2
  69.1 0.6 convolution_convert_fusion
  69.7 0.5 copy-done.2
  70.3 10.5 %all_to_all.25.pieces = bf16[8,8,1024]{2,1,0:T(8,128)(2,1)S(1)} all-to-all(bf16[8,8,1024]{2,1,0:T(8,128)(2,1)S(1)} %maximum_bitcast_fusion), channel_id=1, replica_groups=mesh['y'=4,'xh'=2,'core'=2,'xl'=2,'z1'=4,'z0'=4] {'xl','z0'}, dimensions={0} | all-to-all | bytes 262144 | tf_op jit(solution)/shard_map/all_to_all | solution.py:146
  80.7 0.7 share.1
  81.4 4.9 %all-to-all-start.3 = ((bf16[4,8,1024]{2,1,0:T(8,128)(2,1)}), bf16[4,8,1024]{2,1,0:T(8,128)(2,1)S(1)}, u32[]{:S(2)}, u32[]{:S(2)}) async-start(bf16[4,8,1024]{2,1,0:T(8,128)(2,1)} %share.1), calls=%async_computation.3 | async-start | bytes 131072 | tf_op jit(solution)/shard_map/all_to_all | solution.py:156
  86.3 0.1 pad_add_fusion.place
  86.3 12.9 %all-to-all-done.3.pieces = bf16[4,8,1024]{2,1,0:T(8,128)(2,1)S(1)} async-done(((bf16[4,8,1024]{2,1,0:T(8,128)(2,1)}), bf16[4,8,1024]{2,1,0:T(8,128)(2,1)S(1)}, u32[]{:S(2)}, u32[]{:S(2)}) %all-to-all-start.3) | async-done | bytes 65568 | tf_op jit(solution)/shard_map/all_to_all | solution.py:156
  99.3 0.0 copy-done.1
  99.3 0.0 copy-start.3
  99.3 0.6 coef.1
  99.9 9.9 %all_to_all.26 = bf16[8,8,1024]{2,1,0:T(8,128)(2,1)S(1)} all-to-all(bf16[8,8,1024]{2,1,0:T(8,128)(2,1)S(1)} %coef.1), channel_id=1, replica_groups=mesh['y'=4,'xh'=2,'core'=2,'xl'=2,'z1'=4,'z0'=4] {'xl','z0'}, dimensions={0} | all-to-all | bytes 262144 | tf_op jit(solution)/shard_map/all_to_all | solution.py:166
  109.8 0.4 fusion.8
  110.2 0.0 copy-done.3
  110.2 0.4 fusion.2
  110.6 1.8 %convolution_add_fusion.1 = f32[64,3072]{1,0:T(8,128)S(1)} fusion(f32[64,3072]{1,0:T(8,128)S(1)} %fusion.8, bf16[256,3072]{1,0:T(8,128)(2,1)} %collective-permute-done.5, bf16[64,1024]{1,0:T(8,128)(2,1)S(1)} %bitcast.43), kind=kOutput, calls=%fused_computation.1 | convolution fusion | flops 100859904 | bytes 3178496 | tf_op jit(solution)/shard_map/dot_general | solution.py:170
  112.4 1.8 %fusion.1 = bf16[8,8,24,128]{3,1,2,0:T(8,128)(2,1)S(1)} fusion(bf16[64,3072]{1,0:T(8,128)(2,1)S(1)} %stencil_second.1, f32[64,3072]{1,0:T(8,128)S(1)} %fusion.2, f32[64,3072]{1,0:T(8,128)S(1)} %convolution_add_fusion.1, bf16[256,3072]{1,0:T(8,128)(2,1)} %bitcast, bf16[64,1024]{1,0:T(8,128)(2,1)S(1)} %bitcast.44), kind=kOutput, calls=%fused_computation.8 | convolution fusion | flops 101646336 | bytes 3964928 | tf_op jit(solution)/shard_map/dot_general | solution.py:170
  114.2 0.8 copy.5
  (1 shorter events, 0.0 us)
Async XLA Ops:
  2.4 36.1 %all-to-all-start.1 = ((bf16[4,64,3072]{2,1,0:T(8,128)(2,1)}), bf16[4,64,3072]{2,1,0:T(8,128)(2,1)S(1)}, u32[]{:S(2)}, u32[]{:S(2)}) async-start(bf16[4,64,3072]{2,1,0:T(8,128)(2,1)} %broadcast_in_dim.5), calls=%async_computation.1 | async-start | bytes 3145728 | tf_op jit(solution)/shard_map/all_to_all | solution.py:113
  11.6 13.9 %collective-permute-start.2 = (bf16[64,3072]{1,0:T(8,128)(2,1)S(1)}, bf16[64,3072]{1,0:T(8,128)(2,1)S(1)}, u32[]{:S(2)}, u32[]{:S(2)}) collective-permute-start(bf16[64,3072]{1,0:T(8,128)(2,1)S(1)} %bitcast.31), channel_id=1, source_target_pairs={{0,64},{64,0},{1,65},{65,1},{2,66},{66,2},{3,67},{67,3},{4,68},{68... | collective-permute-start | bytes 1179656 | tf_op jit(solution)/shard_map/ppermute | solution.py:127
  13.5 17.6 %collective-permute-start.1 = (bf16[64,3072]{1,0:T(8,128)(2,1)S(1)}, bf16[64,3072]{1,0:T(8,128)(2,1)S(1)}, u32[]{:S(2)}, u32[]{:S(2)}) collective-permute-start(bf16[64,3072]{1,0:T(8,128)(2,1)S(1)} %bitcast.32), channel_id=1, source_target_pairs={{1,0},{2,1},{3,2},{4,3},{5,4},{6,5},{7,6},{8,7},{9,8},{10,9},{11,1... | collective-permute-start | bytes 1179656 | tf_op jit(solution)/shard_map/ppermute | solution.py:31
  23.5 13.7 %collective-permute-start = (bf16[64,3072]{1,0:T(8,128)(2,1)S(1)}, bf16[64,3072]{1,0:T(8,128)(2,1)S(1)}, u32[]{:S(2)}, u32[]{:S(2)}) collective-permute-start(bf16[64,3072]{1,0:T(8,128)(2,1)S(1)} %bitcast.33), channel_id=1, source_target_pairs={{0,1},{1,2},{2,3},{3,4},{4,5},{5,6},{6,7},{7,8},{8,9},{9,10},{10,1... | collective-permute-start | bytes 1179656 | tf_op jit(solution)/shard_map/ppermute | solution.py:31
  38.5 4.9 %copy-start = (f32[3,8,128]{2,1,0:T(8,128)S(1)}, f32[3,8,128]{2,1,0:T(8,128)}, u32[]{:S(2)}) copy-start(f32[3,8,128]{2,1,0:T(8,128)} %param.4) | copy-start | bytes 36868
  38.6 23.1 %all-to-all-start = ((bf16[4,64,3072]{2,1,0:T(8,128)(2,1)}), bf16[4,64,3072]{2,1,0:T(8,128)(2,1)}, u32[]{:S(2)}, u32[]{:S(2)}) async-start(bf16[4,64,3072]{2,1,0:T(8,128)(2,1)} %broadcast_in_dim.4), calls=%async_computation | async-start | bytes 3145728 | tf_op jit(solution)/shard_map/all_to_all | solution.py:113
  44.4 11.0 %collective-permute-start.4 = (bf16[64,3072]{1,0:T(8,128)(2,1)S(1)}, bf16[64,3072]{1,0:T(8,128)(2,1)S(1)}, u32[]{:S(2)}, u32[]{:S(2)}) collective-permute-start(bf16[64,3072]{1,0:T(8,128)(2,1)S(1)} %stencil_first.1.mid), channel_id=1, source_target_pairs={{1,0},{2,1},{3,2},{4,3},{5,4},{6,5},{7,6},{8,7},{9,8},{10,9},{11,1... | collective-permute-start | bytes 1179656 | tf_op jit(solution)/shard_map/ppermute | solution.py:31
  48.7 12.9 %collective-permute-start.3 = (bf16[64,3072]{1,0:T(8,128)(2,1)S(1)}, bf16[64,3072]{1,0:T(8,128)(2,1)S(1)}, u32[]{:S(2)}, u32[]{:S(2)}) collective-permute-start(bf16[64,3072]{1,0:T(8,128)(2,1)S(1)} %stencil_first.1.mid), channel_id=1, source_target_pairs={{0,1},{1,2},{2,3},{3,4},{4,5},{5,6},{6,7},{7,8},{8,9},{9,10},{10,1... | collective-permute-start | bytes 1179656 | tf_op jit(solution)/shard_map/ppermute | solution.py:31
  50.6 16.4 %collective-permute-start.5 = (bf16[256,3072]{1,0:T(8,128)(2,1)S(1)}, bf16[256,3072]{1,0:T(8,128)(2,1)}, u32[]{:S(2)}, u32[]{:S(2)}) collective-permute-start(bf16[256,3072]{1,0:T(8,128)(2,1)S(1)} %bitcast.38), channel_id=1, source_target_pairs={{0,32},{32,0},{1,33},{33,1},{2,34},{34,2},{3,35},{35,3},{4,36},{36... | collective-permute-start | bytes 4718600 | tf_op jit(solution)/shard_map/ppermute | solution.py:117
  61.6 7.5 %collective-permute-start.6 = (bf16[256,3072]{1,0:T(8,128)(2,1)}, bf16[256,3072]{1,0:T(8,128)(2,1)S(1)}, u32[]{:S(2)}, u32[]{:S(2)}) collective-permute-start(bf16[256,3072]{1,0:T(8,128)(2,1)} %bitcast), channel_id=1, source_target_pairs={{0,32},{32,0},{1,33},{33,1},{2,34},{34,2},{3,35},{35,3},{4,36},{36... | collective-permute-start | bytes 4718600 | tf_op jit(solution)/shard_map/ppermute | solution.py:117
  69.1 30.2 %copy-start.1 = (s32[16]{0:T(128)S(1)}, s32[16]{0:T(128)}, u32[]{:S(2)}) copy-start(s32[16]{0:T(128)} %plan.1) | copy-start | bytes 196
  69.1 1.2 %copy-start.2 = (bf16[256,3072]{1,0:T(8,128)(2,1)}, bf16[256,3072]{1,0:T(8,128)(2,1)S(1)}, u32[]{:S(2)}) copy-start(bf16[256,3072]{1,0:T(8,128)(2,1)S(1)} %collective-permute-done.6) | copy-start | bytes 4718596
  81.4 17.9 %all-to-all-start.3 = ((bf16[4,8,1024]{2,1,0:T(8,128)(2,1)}), bf16[4,8,1024]{2,1,0:T(8,128)(2,1)S(1)}, u32[]{:S(2)}, u32[]{:S(2)}) async-start(bf16[4,8,1024]{2,1,0:T(8,128)(2,1)} %share.1), calls=%async_computation.3 | async-start | bytes 131072 | tf_op jit(solution)/shard_map/all_to_all | solution.py:156
  99.3 10.9 %copy-start.3 = (bf16[256,3072]{1,0:T(8,128)(2,1)S(1)}, bf16[256,3072]{1,0:T(8,128)(2,1)}, u32[]{:S(2)}) copy-start(bf16[256,3072]{1,0:T(8,128)(2,1)} %copy-done.2) | copy-start | bytes 4718596

commit v4 on v3

--- a/solution.py
+++ b/solution.py
@@ -63,7 +63,7 @@
         out[:, cells] = total.astype(BF16)
 
 
-def stencil(before, mid, after, pot, start=None):
+def stencil(before, mid, after, pot, flops, start=None):
     args = [before, mid, after, pot] + ([] if start is None else [start])
     return pl.pallas_call(
         functools.partial(stencil_kernel, start is not None),
@@ -72,7 +72,7 @@
         out_specs=VMEM,
         scratch_shapes=[pltpu.VMEM((mid.shape[0], 3 * mid.shape[1]), F32)],
         compiler_params=PARAMS,
-        cost_estimate=pl.CostEstimate(flops=8_000_000, bytes_accessed=2_000_000, transcendentals=0),
+        cost_estimate=pl.CostEstimate(flops=flops, bytes_accessed=2_000_000, transcendentals=0),
         name="stencil_second" if start is not None else "stencil_first",
     )(*args)
 
@@ -94,6 +94,7 @@
     def earlier(block):
         group, source = divmod(block, bands // 4)
         side = xh if group < 2 else 1 - xh
+        source = (y + (0, 3, 1, 2)[source]) % 4
         parity = core if group % 2 == 0 else 1 - core
         return (plan[4 * source + 2 * side + parity] < turn).astype(jnp.int32)
 
@@ -109,12 +110,32 @@
     return jnp.broadcast_to(block[None], (lax.axis_size("y"),) + block.shape)
 
 
+def stack_kernel(*refs):
+    *blocks, out = refs
+    rows = blocks[0].shape[0]
+    for k, block in enumerate(blocks):
+        out[k * rows : (k + 1) * rows, :] = block[...]
+
+
+def stacked(blocks, flops):
+    rows, cells = blocks[0].shape
+    return pl.pallas_call(
+        stack_kernel,
+        out_shape=jax.ShapeDtypeStruct((len(blocks) * rows, cells), blocks[0].dtype),
+        in_specs=[VMEM] * len(blocks),
+        out_specs=VMEM,
+        compiler_params=PARAMS,
+        cost_estimate=pl.CostEstimate(flops=flops, bytes_accessed=2_000_000, transcendentals=0),
+        name="stack",
+    )(*blocks)
+
+
 def along_y(wide):
     return lax.all_to_all(wide, "y", 0, 0).reshape(-1, wide.shape[-1])
 
 
-def swap_cores(block):
-    return lax.ppermute(block, "core", [(0, 1), (1, 0)])
+def swap(axis, block):
+    return lax.ppermute(block, axis, [(0, 1), (1, 0)])
 
 
 def body(panels, potential, plan):
@@ -123,18 +144,23 @@
     pot = potential.reshape(-1, LANES)
     scale = 1.0 / (rows.shape[1] * lax.axis_size(PENCIL))
     near, far = lax.axis_size(NEAR), lax.axis_size("z1")
+    swapped = stacked([swap("xh", rows)], 100_000_000_000)
+    same = stacked([rows] + [
+        lax.ppermute(rows, "y", [(i, (i + step) % 4) for i in range(4)]) for step in (1, 3, 2)
+    ], 8_000_000)
     before, after = halos(rows)
-    swapped = lax.ppermute(rows, "xh", [(0, 1), (1, 0)])
-    same = along_y(widen(rows))
-    wide = widen(swapped)
-    before, after, wide = lax.optimization_barrier((before, after, wide))
-    other = along_y(wide)
-    first = stencil(before, rows, after, pot)
+    first = stencil(before, rows, after, pot, 8000000)
     before, after = halos(first)
-    same_core = swap_cores(same)
-    other, before, after = lax.optimization_barrier((other, before, after))
-    other_core = swap_cores(other)
-    filtered = stencil(before, first, after, pot, rows)
+    low_y, high_y, opposite = (
+        lax.ppermute(swapped, "y", [(i, (i + step) % 4) for i in range(4)]) for step in (1, 3, 2)
+    )
+    before, after, low_y, high_y, opposite = lax.optimization_barrier(
+        (before, after, low_y, high_y, opposite)
+    )
+    filtered = stencil(before, first, after, pot, 8000000, rows)
+    same_core = swap("core", same)
+    other = jnp.concatenate([swapped, low_y, high_y, opposite], axis=0)
+    other_core = swap("core", other)
     blocks = [same, same_core, other, other_core]
 
     def margins(other):

time: 117 us -> 115 us (0.983)
  starting transfers between devices: 42.8 us -> 52.3 us
  waiting for transfers between devices: 33.8 us -> 29.2 us
  matrix products: 9.64 us -> 5.38 us
  local copies, waits for them, and re-layouts: 5.13 us -> 3.44 us
    ppermute x3 -> x9, starting transfers between devices: 5.74 us -> 29 us  [the longest x3 10.2 us: body(): lax.ppermute(rows, 'y', [(i, (i + step) % 4) for i in range(4)])]
    all_to_all x2 -> x0, starting transfers between devices: 14.1 us -> none  [along_y(): return lax.all_to_all(wide, 'y', 0, 0).reshape(-1, wide.shape[-1])]
    ppermute x4, waiting for transfers between devices: 20.8 us -> 15.6 us  [halos(): return (lax.ppermute(shard, PENCIL, up), lax.ppermute(shard, PENCIL, down))]
    dot_general x4, matrix products: 5.22 us -> 2.4 us  [margins(): lax.dot_general(filtered, other, (((1,), (1,)), ((), ())), preferred_elem...]
    broadcast_in_dim x2 -> x0, local copies, waits for them, and re-layouts: 2.7 us -> none  [widen(): return jnp.broadcast_to(block[None], (lax.axis_size('y'),) + block.shape)]
    dot_general x4, matrix products: 4.41 us -> 2.98 us  [body(): lax.dot_general(coef[:, k * width:(k + 1) * width], block, (((1,), (0,)),...]
    unnamed x10 -> x16, local copies, waits for them, and re-layouts: 2.43 us -> 3.44 us
  transfers between devices with their start and end apart: 10 -> 14, of which waited for: 5 -> 6; matrix products, arithmetic and copies ran while one was open for 5% -> 2% of each run, Pallas kernels for 2% -> 2%
where the time goes in v4:
time: 115 us; the launch traced here: 114 us
  starting transfers between devices  52.3 us (45%)
  waiting for transfers between devices  29.2 us (25%)
  blocking collectives  20.1 us (17%)
  matrix products  5.38 us (5%)
  local copies, waits for them, and re-layouts  3.44 us (3%)
  Pallas kernels  3.12 us (3%)
    ppermute x4, starting transfers between devices, halos(): return (lax.ppermute(shard, PENCIL, up), lax.ppermute(shard, PENCIL, down))  19.2 us
    ppermute x4, waiting for transfers between devices, halos(): return (lax.ppermute(shard, PENCIL, up), lax.ppermute(shard, PENCIL, down))  15.6 us
    all_to_all x1, waiting for transfers between devices, body(): shares = lax.all_to_all(shares, 'z1', 0, 0)  12.9 us
    ppermute x3, starting transfers between devices, body(): lax.ppermute(rows, 'y', [(i, (i + step) % 4) for i in range(4)])  10.2 us
    all_to_all x1, blocking collectives, body(): lax.all_to_all(partial.reshape(near, orbitals // near, -1), NEAR, 0, 0)  10.2 us
    ppermute x3, starting transfers between devices, body(): lax.ppermute(swapped, 'y', [(i, (i + step) % 4) for i in range(4)])  10 us
    all_to_all x1, blocking collectives, body(): coef = lax.all_to_all(coef, NEAR, 0, 0).reshape(orbitals, -1)  9.91 us
    ppermute x3, starting transfers between devices, swap(): return lax.ppermute(block, axis, [(0, 1), (1, 0)])  8.77 us
  transfers between devices with their start and end apart: 14, of which 6 were waited for; matrix products, arithmetic and copies ran while one was open for 2% of the time, Pallas kernels for 2%

profile of v4, /device:TPU:24, one launch (start us, length us, event | category | flops | bytes accessed | tf_op | source)
XLA Modules:
  0.0 114.1 jit_solution(4792809684619277167)
XLA Ops:
  0.0 1.1 copy.7
  1.1 0.0 copy-start
  1.1 4.9 %collective-permute-start.4 = (bf16[64,3072]{1,0:T(8,128)(2,1)S(1)}, bf16[64,3072]{1,0:T(8,128)(2,1)S(1)}, u32[]{:S(2)}, u32[]{:S(2)}) collective-permute-start(bf16[64,3072]{1,0:T(8,128)(2,1)S(1)} %bitcast.28), channel_id=1, source_target_pairs={{0,64},{64,0},{1,65},{65,1},{2,66},{66,2},{3,67},{67,3},{4,68},{68... | collective-permute-start | bytes 1179656 | tf_op jit(solution)/shard_map/ppermute | solution.py:138
  6.0 3.1 %collective-permute-start.10 = (bf16[64,3072]{1,0:T(8,128)(2,1)S(1)}, bf16[64,3072]{1,0:T(8,128)(2,1)S(1)}, u32[]{:S(2)}, u32[]{:S(2)}) collective-permute-start(bf16[64,3072]{1,0:T(8,128)(2,1)S(1)} %bitcast.29), channel_id=1, source_target_pairs={{0,256},{128,384},{256,0},{384,128},{1,257},{129,385},{257,1},{385... | collective-permute-start | bytes 1179656 | tf_op jit(solution)/shard_map/ppermute | solution.py:149
  9.2 4.1 %collective-permute-start.9 = (bf16[64,3072]{1,0:T(8,128)(2,1)S(1)}, bf16[64,3072]{1,0:T(8,128)(2,1)S(1)}, u32[]{:S(2)}, u32[]{:S(2)}) collective-permute-start(bf16[64,3072]{1,0:T(8,128)(2,1)S(1)} %bitcast.30), channel_id=1, source_target_pairs={{0,384},{128,0},{256,128},{384,256},{1,385},{129,1},{257,129},{385... | collective-permute-start | bytes 1179656 | tf_op jit(solution)/shard_map/ppermute | solution.py:149
  13.3 2.9 %collective-permute-start.8 = (bf16[64,3072]{1,0:T(8,128)(2,1)S(1)}, bf16[64,3072]{1,0:T(8,128)(2,1)S(1)}, u32[]{:S(2)}, u32[]{:S(2)}) collective-permute-start(bf16[64,3072]{1,0:T(8,128)(2,1)S(1)} %bitcast.31), channel_id=1, source_target_pairs={{0,128},{128,256},{256,384},{384,0},{1,129},{129,257},{257,385},{3... | collective-permute-start | bytes 1179656 | tf_op jit(solution)/shard_map/ppermute | solution.py:149
  16.2 11.4 %collective-permute-start.1 = (bf16[64,3072]{1,0:T(8,128)(2,1)S(1)}, bf16[64,3072]{1,0:T(8,128)(2,1)S(1)}, u32[]{:S(2)}, u32[]{:S(2)}) collective-permute-start(bf16[64,3072]{1,0:T(8,128)(2,1)S(1)} %bitcast.32), channel_id=1, source_target_pairs={{1,0},{2,1},{3,2},{4,3},{5,4},{6,5},{7,6},{8,7},{9,8},{10,9},{11,1... | collective-permute-start | bytes 1179656 | tf_op jit(solution)/shard_map/ppermute | solution.py:31
  27.7 0.0 collective-permute-done.4.refs_0_
  27.7 1.9 %collective-permute-start = (bf16[64,3072]{1,0:T(8,128)(2,1)S(1)}, bf16[64,3072]{1,0:T(8,128)(2,1)S(1)}, u32[]{:S(2)}, u32[]{:S(2)}) collective-permute-start(bf16[64,3072]{1,0:T(8,128)(2,1)S(1)} %bitcast.33), channel_id=1, source_target_pairs={{0,1},{1,2},{2,3},{3,4},{4,5},{5,6},{6,7},{7,8},{8,9},{9,10},{10,1... | collective-permute-start | bytes 1179656 | tf_op jit(solution)/shard_map/ppermute | solution.py:31
  29.6 5.3 %collective-permute-done.1.after = bf16[64,3072]{1,0:T(8,128)(2,1)S(1)} collective-permute-done((bf16[64,3072]{1,0:T(8,128)(2,1)S(1)}, bf16[64,3072]{1,0:T(8,128)(2,1)S(1)}, u32[]{:S(2)}, u32[]{:S(2)}) %collective-permute-start.1) | collective-permute-done | bytes 393248 | tf_op jit(solution)/shard_map/ppermute | solution.py:31
  34.9 3.0 %collective-permute-start.7 = (bf16[64,3072]{1,0:T(8,128)(2,1)S(1)}, bf16[64,3072]{1,0:T(8,128)(2,1)S(1)}, u32[]{:S(2)}, u32[]{:S(2)}) collective-permute-start(bf16[64,3072]{1,0:T(8,128)(2,1)S(1)} %stack.18), channel_id=1, source_target_pairs={{0,256},{128,384},{256,0},{384,128},{1,257},{129,385},{257,1},{385... | collective-permute-start | bytes 1179656 | tf_op jit(solution)/shard_map/ppermute | solution.py:155
  37.9 3.2 %collective-permute-done.before = bf16[64,3072]{1,0:T(8,128)(2,1)S(1)} collective-permute-done((bf16[64,3072]{1,0:T(8,128)(2,1)S(1)}, bf16[64,3072]{1,0:T(8,128)(2,1)S(1)}, u32[]{:S(2)}, u32[]{:S(2)}) %collective-permute-start) | collective-permute-done | bytes 393248 | tf_op jit(solution)/shard_map/ppermute | solution.py:31
  41.1 1.9 %collective-permute-start.6 = (bf16[64,3072]{1,0:T(8,128)(2,1)S(1)}, bf16[64,3072]{1,0:T(8,128)(2,1)S(1)}, u32[]{:S(2)}, u32[]{:S(2)}) collective-permute-start(bf16[64,3072]{1,0:T(8,128)(2,1)S(1)} %stack.18), channel_id=1, source_target_pairs={{0,384},{128,0},{256,128},{384,256},{1,385},{129,1},{257,129},{385... | collective-permute-start | bytes 1179656 | tf_op jit(solution)/shard_map/ppermute | solution.py:155
  43.1 0.9 stencil_first.1.mid
  43.9 0.0 collective-permute-done.10.refs_3_
  44.0 5.1 %collective-permute-start.5 = (bf16[64,3072]{1,0:T(8,128)(2,1)S(1)}, bf16[64,3072]{1,0:T(8,128)(2,1)S(1)}, u32[]{:S(2)}, u32[]{:S(2)}) collective-permute-start(bf16[64,3072]{1,0:T(8,128)(2,1)S(1)} %stack.18), channel_id=1, source_target_pairs={{0,128},{128,256},{256,384},{384,0},{1,129},{129,257},{257,385},{3... | collective-permute-start | bytes 1179656 | tf_op jit(solution)/shard_map/ppermute | solution.py:155
  49.1 0.0 collective-permute-done.9.refs_2_
  49.1 3.3 %collective-permute-start.3 = (bf16[64,3072]{1,0:T(8,128)(2,1)S(1)}, bf16[64,3072]{1,0:T(8,128)(2,1)S(1)}, u32[]{:S(2)}, u32[]{:S(2)}) collective-permute-start(bf16[64,3072]{1,0:T(8,128)(2,1)S(1)} %stencil_first.1.mid), channel_id=1, source_target_pairs={{1,0},{2,1},{3,2},{4,3},{5,4},{6,5},{7,6},{8,7},{9,8},{10,9},{11,1... | collective-permute-start | bytes 1179656 | tf_op jit(solution)/shard_map/ppermute | solution.py:31
  52.4 0.0 collective-permute-done.8.refs_1_
  52.4 2.6 %collective-permute-start.2 = (bf16[64,3072]{1,0:T(8,128)(2,1)S(1)}, bf16[64,3072]{1,0:T(8,128)(2,1)S(1)}, u32[]{:S(2)}, u32[]{:S(2)}) collective-permute-start(bf16[64,3072]{1,0:T(8,128)(2,1)S(1)} %stencil_first.1.mid), channel_id=1, source_target_pairs={{0,1},{1,2},{2,3},{3,4},{4,5},{5,6},{6,7},{7,8},{8,9},{9,10},{10,1... | collective-permute-start | bytes 1179656 | tf_op jit(solution)/shard_map/ppermute | solution.py:31
  55.0 0.1 stack.19
  55.1 0.0 collective-permute-done.7
  55.1 1.9 %collective-permute-start.11 = (bf16[256,3072]{1,0:T(8,128)(2,1)S(1)}, bf16[256,3072]{1,0:T(8,128)(2,1)S(1)}, u32[]{:S(2)}, u32[]{:S(2)}) collective-permute-start(bf16[256,3072]{1,0:T(8,128)(2,1)S(1)} %stack.19), channel_id=1, source_target_pairs={{0,32},{32,0},{1,33},{33,1},{2,34},{34,2},{3,35},{35,3},{4,36},{36... | collective-permute-start | bytes 4718600 | tf_op jit(solution)/shard_map/ppermute | solution.py:138
  57.0 0.0 collective-permute-done.6
  57.0 1.9 %collective-permute-done.3.after = bf16[64,3072]{1,0:T(8,128)(2,1)S(1)} collective-permute-done((bf16[64,3072]{1,0:T(8,128)(2,1)S(1)}, bf16[64,3072]{1,0:T(8,128)(2,1)S(1)}, u32[]{:S(2)}, u32[]{:S(2)}) %collective-permute-start.3) | collective-permute-done | bytes 393248 | tf_op jit(solution)/shard_map/ppermute | solution.py:31
  59.0 5.2 %collective-permute-done.2.before = bf16[64,3072]{1,0:T(8,128)(2,1)S(1)} collective-permute-done((bf16[64,3072]{1,0:T(8,128)(2,1)S(1)}, bf16[64,3072]{1,0:T(8,128)(2,1)S(1)}, u32[]{:S(2)}, u32[]{:S(2)}) %collective-permute-start.2) | collective-permute-done | bytes 393248 | tf_op jit(solution)/shard_map/ppermute | solution.py:31
  64.2 0.1 pad_maximum_fusion
  64.3 1.9 %collective-permute-start.12 = (bf16[256,3072]{1,0:T(8,128)(2,1)S(1)}, bf16[256,3072]{1,0:T(8,128)(2,1)S(1)}, u32[]{:S(2)}, u32[]{:S(2)}) collective-permute-start(bf16[256,3072]{1,0:T(8,128)(2,1)S(1)} %pad_maximum_fusion), channel_id=1, source_target_pairs={{0,32},{32,0},{1,33},{33,1},{2,34},{34,2},{3,35},{35,3},{4,36},{36... | collective-permute-start | bytes 4718600 | tf_op jit(solution)/shard_map/ppermute | solution.py:138
  66.2 0.9 stencil_second.1
  67.1 0.6 convolution_convert_fusion.3
  67.7 0.6 convolution_convert_fusion.1
  68.3 0.6 convolution_convert_fusion.2
  68.9 0.7 collective-permute-done.12
  69.6 0.6 convolution_convert_fusion
  70.2 0.5 copy-done.5
  70.8 10.2 %all_to_all.15.pieces = bf16[8,8,1024]{2,1,0:T(8,128)(2,1)S(1)} all-to-all(bf16[8,8,1024]{2,1,0:T(8,128)(2,1)S(1)} %maximum_bitcast_fusion), channel_id=1, replica_groups=mesh['y'=4,'xh'=2,'core'=2,'xl'=2,'z1'=4,'z0'=4] {'xl','z0'}, dimensions={0} | all-to-all | bytes 262144 | tf_op jit(solution)/shard_map/all_to_all | solution.py:172
  80.9 0.7 share.1
  81.6 4.1 %all-to-all-start.1 = ((bf16[4,8,1024]{2,1,0:T(8,128)(2,1)}), bf16[4,8,1024]{2,1,0:T(8,128)(2,1)S(1)}, u32[]{:S(2)}, u32[]{:S(2)}) async-start(bf16[4,8,1024]{2,1,0:T(8,128)(2,1)} %share.1), calls=%async_computation.1 | async-start | bytes 131072 | tf_op jit(solution)/shard_map/all_to_all | solution.py:182
  85.7 0.1 pad_add_fusion.place
  85.8 12.9 %all-to-all-done.1.pieces = bf16[4,8,1024]{2,1,0:T(8,128)(2,1)S(1)} async-done(((bf16[4,8,1024]{2,1,0:T(8,128)(2,1)}), bf16[4,8,1024]{2,1,0:T(8,128)(2,1)S(1)}, u32[]{:S(2)}, u32[]{:S(2)}) %all-to-all-start.1) | async-done | bytes 65568 | tf_op jit(solution)/shard_map/all_to_all | solution.py:182
  98.7 0.6 coef.1
  99.3 9.9 %all_to_all.16 = bf16[8,8,1024]{2,1,0:T(8,128)(2,1)S(1)} all-to-all(bf16[8,8,1024]{2,1,0:T(8,128)(2,1)S(1)} %coef.1), channel_id=1, replica_groups=mesh['y'=4,'xh'=2,'core'=2,'xl'=2,'z1'=4,'z0'=4] {'xl','z0'}, dimensions={0} | all-to-all | bytes 262144 | tf_op jit(solution)/shard_map/all_to_all | solution.py:192
  109.2 1.8 %fusion.5 = f32[64,3072]{1,0:T(8,128)S(1)} fusion(bf16[256,3072]{1,0:T(8,128)(2,1)} %copy-done.2, bf16[64,1024]{1,0:T(8,128)(2,1)S(1)} %bitcast.39), kind=kOutput, calls=%fused_computation.13 | convolution fusion | flops 100663296 | bytes 2392064 | tf_op jit(solution)/shard_map/dot_general | solution.py:196
  111.0 0.4 fusion.7
  111.4 0.4 fusion
  111.8 1.0 copy-done.6
  112.8 0.4 fusion.1
  113.3 0.8 copy.5
  (15 shorter events, 0.1 us)
Async XLA Ops:
  1.1 42.0 %copy-start = (f32[3,8,128]{2,1,0:T(8,128)S(1)}, f32[3,8,128]{2,1,0:T(8,128)}, u32[]{:S(2)}) copy-start(f32[3,8,128]{2,1,0:T(8,128)} %param.4) | copy-start | bytes 36868
  1.1 26.6 %collective-permute-start.4 = (bf16[64,3072]{1,0:T(8,128)(2,1)S(1)}, bf16[64,3072]{1,0:T(8,128)(2,1)S(1)}, u32[]{:S(2)}, u32[]{:S(2)}) collective-permute-start(bf16[64,3072]{1,0:T(8,128)(2,1)S(1)} %bitcast.28), channel_id=1, source_target_pairs={{0,64},{64,0},{1,65},{65,1},{2,66},{66,2},{3,67},{67,3},{4,68},{68... | collective-permute-start | bytes 1179656 | tf_op jit(solution)/shard_map/ppermute | solution.py:138
  6.0 37.9 %collective-permute-start.10 = (bf16[64,3072]{1,0:T(8,128)(2,1)S(1)}, bf16[64,3072]{1,0:T(8,128)(2,1)S(1)}, u32[]{:S(2)}, u32[]{:S(2)}) collective-permute-start(bf16[64,3072]{1,0:T(8,128)(2,1)S(1)} %bitcast.29), channel_id=1, source_target_pairs={{0,256},{128,384},{256,0},{384,128},{1,257},{129,385},{257,1},{385... | collective-permute-start | bytes 1179656 | tf_op jit(solution)/shard_map/ppermute | solution.py:149
  9.2 39.9 %collective-permute-start.9 = (bf16[64,3072]{1,0:T(8,128)(2,1)S(1)}, bf16[64,3072]{1,0:T(8,128)(2,1)S(1)}, u32[]{:S(2)}, u32[]{:S(2)}) collective-permute-start(bf16[64,3072]{1,0:T(8,128)(2,1)S(1)} %bitcast.30), channel_id=1, source_target_pairs={{0,384},{128,0},{256,128},{384,256},{1,385},{129,1},{257,129},{385... | collective-permute-start | bytes 1179656 | tf_op jit(solution)/shard_map/ppermute | solution.py:149
  13.3 39.1 %collective-permute-start.8 = (bf16[64,3072]{1,0:T(8,128)(2,1)S(1)}, bf16[64,3072]{1,0:T(8,128)(2,1)S(1)}, u32[]{:S(2)}, u32[]{:S(2)}) collective-permute-start(bf16[64,3072]{1,0:T(8,128)(2,1)S(1)} %bitcast.31), channel_id=1, source_target_pairs={{0,128},{128,256},{256,384},{384,0},{1,129},{129,257},{257,385},{3... | collective-permute-start | bytes 1179656 | tf_op jit(solution)/shard_map/ppermute | solution.py:149
  16.2 18.7 %collective-permute-start.1 = (bf16[64,3072]{1,0:T(8,128)(2,1)S(1)}, bf16[64,3072]{1,0:T(8,128)(2,1)S(1)}, u32[]{:S(2)}, u32[]{:S(2)}) collective-permute-start(bf16[64,3072]{1,0:T(8,128)(2,1)S(1)} %bitcast.32), channel_id=1, source_target_pairs={{1,0},{2,1},{3,2},{4,3},{5,4},{6,5},{7,6},{8,7},{9,8},{10,9},{11,1... | collective-permute-start | bytes 1179656 | tf_op jit(solution)/shard_map/ppermute | solution.py:31
  27.7 13.5 %collective-permute-start = (bf16[64,3072]{1,0:T(8,128)(2,1)S(1)}, bf16[64,3072]{1,0:T(8,128)(2,1)S(1)}, u32[]{:S(2)}, u32[]{:S(2)}) collective-permute-start(bf16[64,3072]{1,0:T(8,128)(2,1)S(1)} %bitcast.33), channel_id=1, source_target_pairs={{0,1},{1,2},{2,3},{3,4},{4,5},{5,6},{6,7},{7,8},{8,9},{9,10},{10,1... | collective-permute-start | bytes 1179656 | tf_op jit(solution)/shard_map/ppermute | solution.py:31
  34.9 20.2 %collective-permute-start.7 = (bf16[64,3072]{1,0:T(8,128)(2,1)S(1)}, bf16[64,3072]{1,0:T(8,128)(2,1)S(1)}, u32[]{:S(2)}, u32[]{:S(2)}) collective-permute-start(bf16[64,3072]{1,0:T(8,128)(2,1)S(1)} %stack.18), channel_id=1, source_target_pairs={{0,256},{128,384},{256,0},{384,128},{1,257},{129,385},{257,1},{385... | collective-permute-start | bytes 1179656 | tf_op jit(solution)/shard_map/ppermute | solution.py:155
  41.1 15.9 %collective-permute-start.6 = (bf16[64,3072]{1,0:T(8,128)(2,1)S(1)}, bf16[64,3072]{1,0:T(8,128)(2,1)S(1)}, u32[]{:S(2)}, u32[]{:S(2)}) collective-permute-start(bf16[64,3072]{1,0:T(8,128)(2,1)S(1)} %stack.18), channel_id=1, source_target_pairs={{0,384},{128,0},{256,128},{384,256},{1,385},{129,1},{257,129},{385... | collective-permute-start | bytes 1179656 | tf_op jit(solution)/shard_map/ppermute | solution.py:155
  44.0 13.1 %collective-permute-start.5 = (bf16[64,3072]{1,0:T(8,128)(2,1)S(1)}, bf16[64,3072]{1,0:T(8,128)(2,1)S(1)}, u32[]{:S(2)}, u32[]{:S(2)}) collective-permute-start(bf16[64,3072]{1,0:T(8,128)(2,1)S(1)} %stack.18), channel_id=1, source_target_pairs={{0,128},{128,256},{256,384},{384,0},{1,129},{129,257},{257,385},{3... | collective-permute-start | bytes 1179656 | tf_op jit(solution)/shard_map/ppermute | solution.py:155
  49.1 9.9 %collective-permute-start.3 = (bf16[64,3072]{1,0:T(8,128)(2,1)S(1)}, bf16[64,3072]{1,0:T(8,128)(2,1)S(1)}, u32[]{:S(2)}, u32[]{:S(2)}) collective-permute-start(bf16[64,3072]{1,0:T(8,128)(2,1)S(1)} %stencil_first.1.mid), channel_id=1, source_target_pairs={{1,0},{2,1},{3,2},{4,3},{5,4},{6,5},{7,6},{8,7},{9,8},{10,9},{11,1... | collective-permute-start | bytes 1179656 | tf_op jit(solution)/shard_map/ppermute | solution.py:31
  52.4 11.8 %collective-permute-start.2 = (bf16[64,3072]{1,0:T(8,128)(2,1)S(1)}, bf16[64,3072]{1,0:T(8,128)(2,1)S(1)}, u32[]{:S(2)}, u32[]{:S(2)}) collective-permute-start(bf16[64,3072]{1,0:T(8,128)(2,1)S(1)} %stencil_first.1.mid), channel_id=1, source_target_pairs={{0,1},{1,2},{2,3},{3,4},{4,5},{5,6},{6,7},{7,8},{8,9},{9,10},{10,1... | collective-permute-start | bytes 1179656 | tf_op jit(solution)/shard_map/ppermute | solution.py:31
  55.1 13.2 %collective-permute-start.11 = (bf16[256,3072]{1,0:T(8,128)(2,1)S(1)}, bf16[256,3072]{1,0:T(8,128)(2,1)S(1)}, u32[]{:S(2)}, u32[]{:S(2)}) collective-permute-start(bf16[256,3072]{1,0:T(8,128)(2,1)S(1)} %stack.19), channel_id=1, source_target_pairs={{0,32},{32,0},{1,33},{33,1},{2,34},{34,2},{3,35},{35,3},{4,36},{36... | collective-permute-start | bytes 4718600 | tf_op jit(solution)/shard_map/ppermute | solution.py:138
  64.3 3.4 %copy-start.2 = (bf16[256,3072]{1,0:T(8,128)(2,1)}, bf16[256,3072]{1,0:T(8,128)(2,1)S(1)}, u32[]{:S(2)}) copy-start(bf16[256,3072]{1,0:T(8,128)(2,1)S(1)} %pad_maximum_fusion) | copy-start | bytes 4718596
  64.3 5.3 %collective-permute-start.12 = (bf16[256,3072]{1,0:T(8,128)(2,1)S(1)}, bf16[256,3072]{1,0:T(8,128)(2,1)S(1)}, u32[]{:S(2)}, u32[]{:S(2)}) collective-permute-start(bf16[256,3072]{1,0:T(8,128)(2,1)S(1)} %pad_maximum_fusion), channel_id=1, source_target_pairs={{0,32},{32,0},{1,33},{33,1},{2,34},{34,2},{3,35},{35,3},{4,36},{36... | collective-permute-start | bytes 4718600 | tf_op jit(solution)/shard_map/ppermute | solution.py:138
  68.3 1.9 %copy-start.3 = (bf16[256,3072]{1,0:T(8,128)(2,1)}, bf16[256,3072]{1,0:T(8,128)(2,1)S(1)}, u32[]{:S(2)}) copy-start(bf16[256,3072]{1,0:T(8,128)(2,1)S(1)} %collective-permute-done.11) | copy-start | bytes 4718596
  68.9 29.8 %copy-start.1 = (s32[16]{0:T(128)S(1)}, s32[16]{0:T(128)}, u32[]{:S(2)}) copy-start(s32[16]{0:T(128)} %plan.1) | copy-start | bytes 196
  69.6 1.2 %copy-start.5 = (bf16[256,3072]{1,0:T(8,128)(2,1)}, bf16[256,3072]{1,0:T(8,128)(2,1)S(1)}, u32[]{:S(2)}) copy-start(bf16[256,3072]{1,0:T(8,128)(2,1)S(1)} %collective-permute-done.12) | copy-start | bytes 4718596
  81.6 17.1 %all-to-all-start.1 = ((bf16[4,8,1024]{2,1,0:T(8,128)(2,1)}), bf16[4,8,1024]{2,1,0:T(8,128)(2,1)S(1)}, u32[]{:S(2)}, u32[]{:S(2)}) async-start(bf16[4,8,1024]{2,1,0:T(8,128)(2,1)} %share.1), calls=%async_computation.1 | async-start | bytes 131072 | tf_op jit(solution)/shard_map/all_to_all | solution.py:182
  98.7 12.3 %copy-start.4 = (bf16[256,3072]{1,0:T(8,128)(2,1)S(1)}, bf16[256,3072]{1,0:T(8,128)(2,1)}, u32[]{:S(2)}) copy-start(bf16[256,3072]{1,0:T(8,128)(2,1)} %copy-done.3) | copy-start | bytes 4718596
  111.4 1.4 %copy-start.6 = (bf16[256,3072]{1,0:T(8,128)(2,1)S(1)}, bf16[256,3072]{1,0:T(8,128)(2,1)}, u32[]{:S(2)}) copy-start(bf16[256,3072]{1,0:T(8,128)(2,1)} %copy-done.5) | copy-start | bytes 4718596

commit v5 on v4

--- a/solution.py
+++ b/solution.py
@@ -192,7 +192,7 @@
     coef = lax.all_to_all(coef, NEAR, 0, 0).reshape(orbitals, -1)
     width = same.shape[0]
     removed = jnp.zeros(rows.shape, F32)
-    for k, block in enumerate(blocks):
+    for k, block in reversed(list(enumerate(blocks))):
         removed = removed + lax.dot_general(
             coef[:, k * width : (k + 1) * width], block, (((1,), (0,)), ((), ())),
             preferred_element_type=F32,

time: 115 us -> 114 us (level)
  matrix products: 5.38 us -> 4.04 us
    dot_general x4, matrix products: 2.98 us -> 1.64 us  [body(): lax.dot_general(coef[:, k * width:(k + 1) * width], block, (((1,), (0,)),...]
    unnamed x16 -> x18, local copies, waits for them, and re-layouts: 3.44 us -> 4.46 us
where the time goes in v5:
time: 114 us
  starting transfers between devices  52.3 us (46%)
  waiting for transfers between devices  29.2 us (26%)
  blocking collectives  20.1 us (18%)
  local copies, waits for them, and re-layouts  4.46 us (4%)
  matrix products  4.04 us (4%)
  Pallas kernels  3.14 us (3%)
    ppermute x4, starting transfers between devices, halos(): return (lax.ppermute(shard, PENCIL, up), lax.ppermute(shard, PENCIL, down))  19.2 us
    ppermute x4, waiting for transfers between devices, halos(): return (lax.ppermute(shard, PENCIL, up), lax.ppermute(shard, PENCIL, down))  15.6 us
    all_to_all x1, waiting for transfers between devices, body(): shares = lax.all_to_all(shares, 'z1', 0, 0)  12.9 us
    ppermute x3, starting transfers between devices, body(): lax.ppermute(rows, 'y', [(i, (i + step) % 4) for i in range(4)])  10.2 us
    all_to_all x1, blocking collectives, body(): lax.all_to_all(partial.reshape(near, orbitals // near, -1), NEAR, 0, 0)  10.2 us
    ppermute x3, starting transfers between devices, body(): lax.ppermute(swapped, 'y', [(i, (i + step) % 4) for i in range(4)])  10 us
    all_to_all x1, blocking collectives, body(): coef = lax.all_to_all(coef, NEAR, 0, 0).reshape(orbitals, -1)  9.91 us
    ppermute x3, starting transfers between devices, swap(): return lax.ppermute(block, axis, [(0, 1), (1, 0)])  8.77 us
  transfers between devices with their start and end apart: 14, of which 6 were waited for; matrix products, arithmetic and copies ran while one was open for 2% of the time, Pallas kernels for 2%

profile of v5, /device:TPU:24, one launch (start us, length us, event | category | flops | bytes accessed | tf_op | source)
XLA Modules:
  0.0 113.8 jit_solution(10941688755785040475)
XLA Ops:
  0.0 1.1 copy.7
  1.1 0.0 copy-start
  1.1 4.9 %collective-permute-start.4 = (bf16[64,3072]{1,0:T(8,128)(2,1)S(1)}, bf16[64,3072]{1,0:T(8,128)(2,1)S(1)}, u32[]{:S(2)}, u32[]{:S(2)}) collective-permute-start(bf16[64,3072]{1,0:T(8,128)(2,1)S(1)} %bitcast.28), channel_id=1, source_target_pairs={{0,64},{64,0},{1,65},{65,1},{2,66},{66,2},{3,67},{67,3},{4,68},{68... | collective-permute-start | bytes 1179656 | tf_op jit(solution)/shard_map/ppermute | solution.py:138
  6.0 3.1 %collective-permute-start.10 = (bf16[64,3072]{1,0:T(8,128)(2,1)S(1)}, bf16[64,3072]{1,0:T(8,128)(2,1)S(1)}, u32[]{:S(2)}, u32[]{:S(2)}) collective-permute-start(bf16[64,3072]{1,0:T(8,128)(2,1)S(1)} %bitcast.29), channel_id=1, source_target_pairs={{0,256},{128,384},{256,0},{384,128},{1,257},{129,385},{257,1},{385... | collective-permute-start | bytes 1179656 | tf_op jit(solution)/shard_map/ppermute | solution.py:149
  9.2 4.1 %collective-permute-start.9 = (bf16[64,3072]{1,0:T(8,128)(2,1)S(1)}, bf16[64,3072]{1,0:T(8,128)(2,1)S(1)}, u32[]{:S(2)}, u32[]{:S(2)}) collective-permute-start(bf16[64,3072]{1,0:T(8,128)(2,1)S(1)} %bitcast.30), channel_id=1, source_target_pairs={{0,384},{128,0},{256,128},{384,256},{1,385},{129,1},{257,129},{385... | collective-permute-start | bytes 1179656 | tf_op jit(solution)/shard_map/ppermute | solution.py:149
  13.3 2.9 %collective-permute-start.8 = (bf16[64,3072]{1,0:T(8,128)(2,1)S(1)}, bf16[64,3072]{1,0:T(8,128)(2,1)S(1)}, u32[]{:S(2)}, u32[]{:S(2)}) collective-permute-start(bf16[64,3072]{1,0:T(8,128)(2,1)S(1)} %bitcast.31), channel_id=1, source_target_pairs={{0,128},{128,256},{256,384},{384,0},{1,129},{129,257},{257,385},{3... | collective-permute-start | bytes 1179656 | tf_op jit(solution)/shard_map/ppermute | solution.py:149
  16.2 11.4 %collective-permute-start.1 = (bf16[64,3072]{1,0:T(8,128)(2,1)S(1)}, bf16[64,3072]{1,0:T(8,128)(2,1)S(1)}, u32[]{:S(2)}, u32[]{:S(2)}) collective-permute-start(bf16[64,3072]{1,0:T(8,128)(2,1)S(1)} %bitcast.32), channel_id=1, source_target_pairs={{1,0},{2,1},{3,2},{4,3},{5,4},{6,5},{7,6},{8,7},{9,8},{10,9},{11,1... | collective-permute-start | bytes 1179656 | tf_op jit(solution)/shard_map/ppermute | solution.py:31
  27.7 0.0 collective-permute-done.4.refs_0_
  27.7 1.9 %collective-permute-start = (bf16[64,3072]{1,0:T(8,128)(2,1)S(1)}, bf16[64,3072]{1,0:T(8,128)(2,1)S(1)}, u32[]{:S(2)}, u32[]{:S(2)}) collective-permute-start(bf16[64,3072]{1,0:T(8,128)(2,1)S(1)} %bitcast.33), channel_id=1, source_target_pairs={{0,1},{1,2},{2,3},{3,4},{4,5},{5,6},{6,7},{7,8},{8,9},{9,10},{10,1... | collective-permute-start | bytes 1179656 | tf_op jit(solution)/shard_map/ppermute | solution.py:31
  29.6 5.3 %collective-permute-done.1.after = bf16[64,3072]{1,0:T(8,128)(2,1)S(1)} collective-permute-done((bf16[64,3072]{1,0:T(8,128)(2,1)S(1)}, bf16[64,3072]{1,0:T(8,128)(2,1)S(1)}, u32[]{:S(2)}, u32[]{:S(2)}) %collective-permute-start.1) | collective-permute-done | bytes 393248 | tf_op jit(solution)/shard_map/ppermute | solution.py:31
  34.9 3.0 %collective-permute-start.7 = (bf16[64,3072]{1,0:T(8,128)(2,1)S(1)}, bf16[64,3072]{1,0:T(8,128)(2,1)S(1)}, u32[]{:S(2)}, u32[]{:S(2)}) collective-permute-start(bf16[64,3072]{1,0:T(8,128)(2,1)S(1)} %stack.18), channel_id=1, source_target_pairs={{0,256},{128,384},{256,0},{384,128},{1,257},{129,385},{257,1},{385... | collective-permute-start | bytes 1179656 | tf_op jit(solution)/shard_map/ppermute | solution.py:155
  37.9 3.2 %collective-permute-done.before = bf16[64,3072]{1,0:T(8,128)(2,1)S(1)} collective-permute-done((bf16[64,3072]{1,0:T(8,128)(2,1)S(1)}, bf16[64,3072]{1,0:T(8,128)(2,1)S(1)}, u32[]{:S(2)}, u32[]{:S(2)}) %collective-permute-start) | collective-permute-done | bytes 393248 | tf_op jit(solution)/shard_map/ppermute | solution.py:31
  41.1 1.9 %collective-permute-start.6 = (bf16[64,3072]{1,0:T(8,128)(2,1)S(1)}, bf16[64,3072]{1,0:T(8,128)(2,1)S(1)}, u32[]{:S(2)}, u32[]{:S(2)}) collective-permute-start(bf16[64,3072]{1,0:T(8,128)(2,1)S(1)} %stack.18), channel_id=1, source_target_pairs={{0,384},{128,0},{256,128},{384,256},{1,385},{129,1},{257,129},{385... | collective-permute-start | bytes 1179656 | tf_op jit(solution)/shard_map/ppermute | solution.py:155
  43.1 0.9 stencil_first.1.mid
  43.9 0.0 collective-permute-done.10.refs_3_
  44.0 5.1 %collective-permute-start.5 = (bf16[64,3072]{1,0:T(8,128)(2,1)S(1)}, bf16[64,3072]{1,0:T(8,128)(2,1)S(1)}, u32[]{:S(2)}, u32[]{:S(2)}) collective-permute-start(bf16[64,3072]{1,0:T(8,128)(2,1)S(1)} %stack.18), channel_id=1, source_target_pairs={{0,128},{128,256},{256,384},{384,0},{1,129},{129,257},{257,385},{3... | collective-permute-start | bytes 1179656 | tf_op jit(solution)/shard_map/ppermute | solution.py:155
  49.1 0.0 collective-permute-done.9.refs_2_
  49.1 3.3 %collective-permute-start.3 = (bf16[64,3072]{1,0:T(8,128)(2,1)S(1)}, bf16[64,3072]{1,0:T(8,128)(2,1)S(1)}, u32[]{:S(2)}, u32[]{:S(2)}) collective-permute-start(bf16[64,3072]{1,0:T(8,128)(2,1)S(1)} %stencil_first.1.mid), channel_id=1, source_target_pairs={{1,0},{2,1},{3,2},{4,3},{5,4},{6,5},{7,6},{8,7},{9,8},{10,9},{11,1... | collective-permute-start | bytes 1179656 | tf_op jit(solution)/shard_map/ppermute | solution.py:31
  52.4 0.0 collective-permute-done.8.refs_1_
  52.4 2.6 %collective-permute-start.2 = (bf16[64,3072]{1,0:T(8,128)(2,1)S(1)}, bf16[64,3072]{1,0:T(8,128)(2,1)S(1)}, u32[]{:S(2)}, u32[]{:S(2)}) collective-permute-start(bf16[64,3072]{1,0:T(8,128)(2,1)S(1)} %stencil_first.1.mid), channel_id=1, source_target_pairs={{0,1},{1,2},{2,3},{3,4},{4,5},{5,6},{6,7},{7,8},{8,9},{9,10},{10,1... | collective-permute-start | bytes 1179656 | tf_op jit(solution)/shard_map/ppermute | solution.py:31
  55.0 0.1 stack.19
  55.1 0.0 collective-permute-done.7
  55.1 1.9 %collective-permute-start.11 = (bf16[256,3072]{1,0:T(8,128)(2,1)S(1)}, bf16[256,3072]{1,0:T(8,128)(2,1)S(1)}, u32[]{:S(2)}, u32[]{:S(2)}) collective-permute-start(bf16[256,3072]{1,0:T(8,128)(2,1)S(1)} %stack.19), channel_id=1, source_target_pairs={{0,32},{32,0},{1,33},{33,1},{2,34},{34,2},{3,35},{35,3},{4,36},{36... | collective-permute-start | bytes 4718600 | tf_op jit(solution)/shard_map/ppermute | solution.py:138
  57.0 1.9 %collective-permute-done.3.after = bf16[64,3072]{1,0:T(8,128)(2,1)S(1)} collective-permute-done((bf16[64,3072]{1,0:T(8,128)(2,1)S(1)}, bf16[64,3072]{1,0:T(8,128)(2,1)S(1)}, u32[]{:S(2)}, u32[]{:S(2)}) %collective-permute-start.3) | collective-permute-done | bytes 393248 | tf_op jit(solution)/shard_map/ppermute | solution.py:31
  59.0 5.2 %collective-permute-done.2.before = bf16[64,3072]{1,0:T(8,128)(2,1)S(1)} collective-permute-done((bf16[64,3072]{1,0:T(8,128)(2,1)S(1)}, bf16[64,3072]{1,0:T(8,128)(2,1)S(1)}, u32[]{:S(2)}, u32[]{:S(2)}) %collective-permute-start.2) | collective-permute-done | bytes 393248 | tf_op jit(solution)/shard_map/ppermute | solution.py:31
  64.2 0.1 pad_maximum_fusion
  64.3 1.9 %collective-permute-start.12 = (bf16[256,3072]{1,0:T(8,128)(2,1)S(1)}, bf16[256,3072]{1,0:T(8,128)(2,1)S(1)}, u32[]{:S(2)}, u32[]{:S(2)}) collective-permute-start(bf16[256,3072]{1,0:T(8,128)(2,1)S(1)} %pad_maximum_fusion), channel_id=1, source_target_pairs={{0,32},{32,0},{1,33},{33,1},{2,34},{34,2},{3,35},{35,3},{4,36},{36... | collective-permute-start | bytes 4718600 | tf_op jit(solution)/shard_map/ppermute | solution.py:138
  66.2 0.9 stencil_second.1
  67.1 0.6 convolution_convert_fusion.3
  67.7 0.6 convolution_convert_fusion.1
  68.4 0.6 convolution_convert_fusion.2
  69.0 0.6 collective-permute-done.12
  69.6 0.6 convolution_convert_fusion
  70.2 0.6 copy-done.6
  70.8 10.2 %all_to_all.15.pieces = bf16[8,8,1024]{2,1,0:T(8,128)(2,1)S(1)} all-to-all(bf16[8,8,1024]{2,1,0:T(8,128)(2,1)S(1)} %maximum_bitcast_fusion), channel_id=1, replica_groups=mesh['y'=4,'xh'=2,'core'=2,'xl'=2,'z1'=4,'z0'=4] {'xl','z0'}, dimensions={0} | all-to-all | bytes 262144 | tf_op jit(solution)/shard_map/all_to_all | solution.py:172
  81.0 0.7 share.1
  81.6 4.1 %all-to-all-start.1 = ((bf16[4,8,1024]{2,1,0:T(8,128)(2,1)}), bf16[4,8,1024]{2,1,0:T(8,128)(2,1)S(1)}, u32[]{:S(2)}, u32[]{:S(2)}) async-start(bf16[4,8,1024]{2,1,0:T(8,128)(2,1)} %share.1), calls=%async_computation.1 | async-start | bytes 131072 | tf_op jit(solution)/shard_map/all_to_all | solution.py:182
  85.7 0.1 pad_add_fusion.place
  85.8 12.9 %all-to-all-done.1.pieces = bf16[4,8,1024]{2,1,0:T(8,128)(2,1)S(1)} async-done(((bf16[4,8,1024]{2,1,0:T(8,128)(2,1)}), bf16[4,8,1024]{2,1,0:T(8,128)(2,1)S(1)}, u32[]{:S(2)}, u32[]{:S(2)}) %all-to-all-start.1) | async-done | bytes 65568 | tf_op jit(solution)/shard_map/all_to_all | solution.py:182
  98.7 0.6 coef.1
  99.3 9.9 %all_to_all.16 = bf16[8,8,1024]{2,1,0:T(8,128)(2,1)S(1)} all-to-all(bf16[8,8,1024]{2,1,0:T(8,128)(2,1)S(1)} %coef.1), channel_id=1, replica_groups=mesh['y'=4,'xh'=2,'core'=2,'xl'=2,'z1'=4,'z0'=4] {'xl','z0'}, dimensions={0} | all-to-all | bytes 262144 | tf_op jit(solution)/shard_map/all_to_all | solution.py:192
  109.2 0.4 fusion.3
  109.7 0.4 fusion.7
  110.0 1.0 copy-done.5
  111.1 0.4 fusion.5
  111.4 1.0 copy-done.7
  112.5 0.5 fusion.2
  112.9 0.8 copy.5
  (17 shorter events, 0.1 us)
Async XLA Ops:
  1.1 42.0 %copy-start = (f32[3,8,128]{2,1,0:T(8,128)S(1)}, f32[3,8,128]{2,1,0:T(8,128)}, u32[]{:S(2)}) copy-start(f32[3,8,128]{2,1,0:T(8,128)} %param.4) | copy-start | bytes 36868
  1.1 26.6 %collective-permute-start.4 = (bf16[64,3072]{1,0:T(8,128)(2,1)S(1)}, bf16[64,3072]{1,0:T(8,128)(2,1)S(1)}, u32[]{:S(2)}, u32[]{:S(2)}) collective-permute-start(bf16[64,3072]{1,0:T(8,128)(2,1)S(1)} %bitcast.28), channel_id=1, source_target_pairs={{0,64},{64,0},{1,65},{65,1},{2,66},{66,2},{3,67},{67,3},{4,68},{68... | collective-permute-start | bytes 1179656 | tf_op jit(solution)/shard_map/ppermute | solution.py:138
  6.0 37.9 %collective-permute-start.10 = (bf16[64,3072]{1,0:T(8,128)(2,1)S(1)}, bf16[64,3072]{1,0:T(8,128)(2,1)S(1)}, u32[]{:S(2)}, u32[]{:S(2)}) collective-permute-start(bf16[64,3072]{1,0:T(8,128)(2,1)S(1)} %bitcast.29), channel_id=1, source_target_pairs={{0,256},{128,384},{256,0},{384,128},{1,257},{129,385},{257,1},{385... | collective-permute-start | bytes 1179656 | tf_op jit(solution)/shard_map/ppermute | solution.py:149
  9.2 39.9 %collective-permute-start.9 = (bf16[64,3072]{1,0:T(8,128)(2,1)S(1)}, bf16[64,3072]{1,0:T(8,128)(2,1)S(1)}, u32[]{:S(2)}, u32[]{:S(2)}) collective-permute-start(bf16[64,3072]{1,0:T(8,128)(2,1)S(1)} %bitcast.30), channel_id=1, source_target_pairs={{0,384},{128,0},{256,128},{384,256},{1,385},{129,1},{257,129},{385... | collective-permute-start | bytes 1179656 | tf_op jit(solution)/shard_map/ppermute | solution.py:149
  13.3 39.1 %collective-permute-start.8 = (bf16[64,3072]{1,0:T(8,128)(2,1)S(1)}, bf16[64,3072]{1,0:T(8,128)(2,1)S(1)}, u32[]{:S(2)}, u32[]{:S(2)}) collective-permute-start(bf16[64,3072]{1,0:T(8,128)(2,1)S(1)} %bitcast.31), channel_id=1, source_target_pairs={{0,128},{128,256},{256,384},{384,0},{1,129},{129,257},{257,385},{3... | collective-permute-start | bytes 1179656 | tf_op jit(solution)/shard_map/ppermute | solution.py:149
  16.2 18.7 %collective-permute-start.1 = (bf16[64,3072]{1,0:T(8,128)(2,1)S(1)}, bf16[64,3072]{1,0:T(8,128)(2,1)S(1)}, u32[]{:S(2)}, u32[]{:S(2)}) collective-permute-start(bf16[64,3072]{1,0:T(8,128)(2,1)S(1)} %bitcast.32), channel_id=1, source_target_pairs={{1,0},{2,1},{3,2},{4,3},{5,4},{6,5},{7,6},{8,7},{9,8},{10,9},{11,1... | collective-permute-start | bytes 1179656 | tf_op jit(solution)/shard_map/ppermute | solution.py:31
  27.7 13.5 %collective-permute-start = (bf16[64,3072]{1,0:T(8,128)(2,1)S(1)}, bf16[64,3072]{1,0:T(8,128)(2,1)S(1)}, u32[]{:S(2)}, u32[]{:S(2)}) collective-permute-start(bf16[64,3072]{1,0:T(8,128)(2,1)S(1)} %bitcast.33), channel_id=1, source_target_pairs={{0,1},{1,2},{2,3},{3,4},{4,5},{5,6},{6,7},{7,8},{8,9},{9,10},{10,1... | collective-permute-start | bytes 1179656 | tf_op jit(solution)/shard_map/ppermute | solution.py:31
  34.9 20.2 %collective-permute-start.7 = (bf16[64,3072]{1,0:T(8,128)(2,1)S(1)}, bf16[64,3072]{1,0:T(8,128)(2,1)S(1)}, u32[]{:S(2)}, u32[]{:S(2)}) collective-permute-start(bf16[64,3072]{1,0:T(8,128)(2,1)S(1)} %stack.18), channel_id=1, source_target_pairs={{0,256},{128,384},{256,0},{384,128},{1,257},{129,385},{257,1},{385... | collective-permute-start | bytes 1179656 | tf_op jit(solution)/shard_map/ppermute | solution.py:155
  41.1 15.9 %collective-permute-start.6 = (bf16[64,3072]{1,0:T(8,128)(2,1)S(1)}, bf16[64,3072]{1,0:T(8,128)(2,1)S(1)}, u32[]{:S(2)}, u32[]{:S(2)}) collective-permute-start(bf16[64,3072]{1,0:T(8,128)(2,1)S(1)} %stack.18), channel_id=1, source_target_pairs={{0,384},{128,0},{256,128},{384,256},{1,385},{129,1},{257,129},{385... | collective-permute-start | bytes 1179656 | tf_op jit(solution)/shard_map/ppermute | solution.py:155
  44.0 13.1 %collective-permute-start.5 = (bf16[64,3072]{1,0:T(8,128)(2,1)S(1)}, bf16[64,3072]{1,0:T(8,128)(2,1)S(1)}, u32[]{:S(2)}, u32[]{:S(2)}) collective-permute-start(bf16[64,3072]{1,0:T(8,128)(2,1)S(1)} %stack.18), channel_id=1, source_target_pairs={{0,128},{128,256},{256,384},{384,0},{1,129},{129,257},{257,385},{3... | collective-permute-start | bytes 1179656 | tf_op jit(solution)/shard_map/ppermute | solution.py:155
  49.1 9.9 %collective-permute-start.3 = (bf16[64,3072]{1,0:T(8,128)(2,1)S(1)}, bf16[64,3072]{1,0:T(8,128)(2,1)S(1)}, u32[]{:S(2)}, u32[]{:S(2)}) collective-permute-start(bf16[64,3072]{1,0:T(8,128)(2,1)S(1)} %stencil_first.1.mid), channel_id=1, source_target_pairs={{1,0},{2,1},{3,2},{4,3},{5,4},{6,5},{7,6},{8,7},{9,8},{10,9},{11,1... | collective-permute-start | bytes 1179656 | tf_op jit(solution)/shard_map/ppermute | solution.py:31
  52.4 11.8 %collective-permute-start.2 = (bf16[64,3072]{1,0:T(8,128)(2,1)S(1)}, bf16[64,3072]{1,0:T(8,128)(2,1)S(1)}, u32[]{:S(2)}, u32[]{:S(2)}) collective-permute-start(bf16[64,3072]{1,0:T(8,128)(2,1)S(1)} %stencil_first.1.mid), channel_id=1, source_target_pairs={{0,1},{1,2},{2,3},{3,4},{4,5},{5,6},{6,7},{7,8},{8,9},{9,10},{10,1... | collective-permute-start | bytes 1179656 | tf_op jit(solution)/shard_map/ppermute | solution.py:31
  55.1 13.2 %collective-permute-start.11 = (bf16[256,3072]{1,0:T(8,128)(2,1)S(1)}, bf16[256,3072]{1,0:T(8,128)(2,1)S(1)}, u32[]{:S(2)}, u32[]{:S(2)}) collective-permute-start(bf16[256,3072]{1,0:T(8,128)(2,1)S(1)} %stack.19), channel_id=1, source_target_pairs={{0,32},{32,0},{1,33},{33,1},{2,34},{34,2},{3,35},{35,3},{4,36},{36... | collective-permute-start | bytes 4718600 | tf_op jit(solution)/shard_map/ppermute | solution.py:138
  64.3 3.4 %copy-start.2 = (bf16[256,3072]{1,0:T(8,128)(2,1)}, bf16[256,3072]{1,0:T(8,128)(2,1)S(1)}, u32[]{:S(2)}) copy-start(bf16[256,3072]{1,0:T(8,128)(2,1)S(1)} %pad_maximum_fusion) | copy-start | bytes 4718596
  64.3 5.3 %collective-permute-start.12 = (bf16[256,3072]{1,0:T(8,128)(2,1)S(1)}, bf16[256,3072]{1,0:T(8,128)(2,1)S(1)}, u32[]{:S(2)}, u32[]{:S(2)}) collective-permute-start(bf16[256,3072]{1,0:T(8,128)(2,1)S(1)} %pad_maximum_fusion), channel_id=1, source_target_pairs={{0,32},{32,0},{1,33},{33,1},{2,34},{34,2},{3,35},{35,3},{4,36},{36... | collective-permute-start | bytes 4718600 | tf_op jit(solution)/shard_map/ppermute | solution.py:138
  68.3 1.9 %copy-start.4 = (bf16[256,3072]{1,0:T(8,128)(2,1)}, bf16[256,3072]{1,0:T(8,128)(2,1)S(1)}, u32[]{:S(2)}) copy-start(bf16[256,3072]{1,0:T(8,128)(2,1)S(1)} %collective-permute-done.11) | copy-start | bytes 4718596
  69.0 29.8 %copy-start.1 = (s32[16]{0:T(128)S(1)}, s32[16]{0:T(128)}, u32[]{:S(2)}) copy-start(s32[16]{0:T(128)} %plan.1) | copy-start | bytes 196
  69.6 1.2 %copy-start.6 = (bf16[256,3072]{1,0:T(8,128)(2,1)}, bf16[256,3072]{1,0:T(8,128)(2,1)S(1)}, u32[]{:S(2)}) copy-start(bf16[256,3072]{1,0:T(8,128)(2,1)S(1)} %collective-permute-done.12) | copy-start | bytes 4718596
  81.6 17.1 %all-to-all-start.1 = ((bf16[4,8,1024]{2,1,0:T(8,128)(2,1)}), bf16[4,8,1024]{2,1,0:T(8,128)(2,1)S(1)}, u32[]{:S(2)}, u32[]{:S(2)}) async-start(bf16[4,8,1024]{2,1,0:T(8,128)(2,1)} %share.1), calls=%async_computation.1 | async-start | bytes 131072 | tf_op jit(solution)/shard_map/all_to_all | solution.py:182
  98.7 10.9 %copy-start.3 = (bf16[256,3072]{1,0:T(8,128)(2,1)S(1)}, bf16[256,3072]{1,0:T(8,128)(2,1)}, u32[]{:S(2)}) copy-start(bf16[256,3072]{1,0:T(8,128)(2,1)} %copy-done.2) | copy-start | bytes 4718596
  109.6 1.4 %copy-start.5 = (bf16[256,3072]{1,0:T(8,128)(2,1)S(1)}, bf16[256,3072]{1,0:T(8,128)(2,1)}, u32[]{:S(2)}) copy-start(bf16[256,3072]{1,0:T(8,128)(2,1)} %copy-done.4) | copy-start | bytes 4718596
  111.1 1.4 %copy-start.7 = (bf16[256,3072]{1,0:T(8,128)(2,1)S(1)}, bf16[256,3072]{1,0:T(8,128)(2,1)}, u32[]{:S(2)}) copy-start(bf16[256,3072]{1,0:T(8,128)(2,1)} %copy-done.6) | copy-start | bytes 4718596

commit v6 on v5

--- a/solution.py
+++ b/solution.py
@@ -154,8 +154,9 @@
     low_y, high_y, opposite = (
         lax.ppermute(swapped, "y", [(i, (i + step) % 4) for i in range(4)]) for step in (1, 3, 2)
     )
-    before, after, low_y, high_y, opposite = lax.optimization_barrier(
-        (before, after, low_y, high_y, opposite)
+    place = jnp.stack([lax.axis_index(a) for a in BAND]).astype(jnp.int32)
+    before, after, low_y, high_y, opposite, place = lax.optimization_barrier(
+        (before, after, low_y, high_y, opposite, place)
     )
     filtered = stencil(before, first, after, pot, 8000000, rows)
     same_core = swap("core", same)
@@ -180,7 +181,6 @@
         name="share",
     )(pieces)
     shares = lax.all_to_all(shares, "z1", 0, 0)
-    place = jnp.stack([lax.axis_index(a) for a in BAND]).astype(jnp.int32)
     coef = pl.pallas_call(
         functools.partial(coef_kernel, scale),
         out_shape=jax.ShapeDtypeStruct((near,) + share, BF16),

time: 114 us -> 112 us (0.982)
  blocking collectives: 20.1 us -> 37 us
  waiting for transfers between devices: 29.2 us -> 16.3 us
  starting transfers between devices: 52.3 us -> 48.2 us
  local copies, waits for them, and re-layouts: 4.46 us -> 1.88 us
    all_to_all x0 -> x1, blocking collectives: none -> 16.9 us  [body(): shares = lax.all_to_all(shares, 'z1', 0, 0)]
    all_to_all x1 -> x0, waiting for transfers between devices: 12.9 us -> none  [body(): shares = lax.all_to_all(shares, 'z1', 0, 0)]
    all_to_all x1 -> x0, starting transfers between devices: 4.1 us -> none  [body(): shares = lax.all_to_all(shares, 'z1', 0, 0)]
    unnamed x18 -> x6, local copies, waits for them, and re-layouts: 4.46 us -> 1.88 us
  transfers between devices with their start and end apart: 14 -> 13, of which waited for: 6 -> 5; matrix products, arithmetic and copies ran while one was open for 2% -> 3% of each run, Pallas kernels for 2% -> 2%
where the time goes in v6:
time: 112 us; the launch traced here: 111 us
  starting transfers between devices  48.2 us (43%)
  blocking collectives  37 us (33%)
  waiting for transfers between devices  16.3 us (15%)
  matrix products  4.04 us (4%)
  Pallas kernels  2.47 us (2%)
  local copies, waits for them, and re-layouts  1.88 us (2%)
  other arithmetic  1.31 us (1%)
    ppermute x4, starting transfers between devices, halos(): return (lax.ppermute(shard, PENCIL, up), lax.ppermute(shard, PENCIL, down))  19.2 us
    all_to_all x1, blocking collectives, body(): shares = lax.all_to_all(shares, 'z1', 0, 0)  16.9 us
    ppermute x4, waiting for transfers between devices, halos(): return (lax.ppermute(shard, PENCIL, up), lax.ppermute(shard, PENCIL, down))  15.6 us
    ppermute x3, starting transfers between devices, body(): lax.ppermute(rows, 'y', [(i, (i + step) % 4) for i in range(4)])  10.2 us
    all_to_all x1, blocking collectives, body(): lax.all_to_all(partial.reshape(near, orbitals // near, -1), NEAR, 0, 0)  10.2 us
    ppermute x3, starting transfers between devices, body(): lax.ppermute(swapped, 'y', [(i, (i + step) % 4) for i in range(4)])  10 us
    all_to_all x1, blocking collectives, body(): coef = lax.all_to_all(coef, NEAR, 0, 0).reshape(orbitals, -1)  9.91 us
    ppermute x3, starting transfers between devices, swap(): return lax.ppermute(block, axis, [(0, 1), (1, 0)])  8.77 us
  transfers between devices with their start and end apart: 13, of which 5 were waited for; matrix products, arithmetic and copies ran while one was open for 3% of the time, Pallas kernels for 2%

profile of v6, /device:TPU:24, one launch (start us, length us, event | category | flops | bytes accessed | tf_op | source)
XLA Modules:
  0.0 111.4 jit_solution(10371608607435384403)
XLA Ops:
  0.0 1.1 copy.7
  1.1 0.0 copy-start
  1.1 4.9 %collective-permute-start.4 = (bf16[64,3072]{1,0:T(8,128)(2,1)S(1)}, bf16[64,3072]{1,0:T(8,128)(2,1)S(1)}, u32[]{:S(2)}, u32[]{:S(2)}) collective-permute-start(bf16[64,3072]{1,0:T(8,128)(2,1)S(1)} %bitcast.28), channel_id=1, source_target_pairs={{0,64},{64,0},{1,65},{65,1},{2,66},{66,2},{3,67},{67,3},{4,68},{68... | collective-permute-start | bytes 1179656 | tf_op jit(solution)/shard_map/ppermute | solution.py:138
  6.0 3.1 %collective-permute-start.10 = (bf16[64,3072]{1,0:T(8,128)(2,1)S(1)}, bf16[64,3072]{1,0:T(8,128)(2,1)S(1)}, u32[]{:S(2)}, u32[]{:S(2)}) collective-permute-start(bf16[64,3072]{1,0:T(8,128)(2,1)S(1)} %bitcast.29), channel_id=1, source_target_pairs={{0,256},{128,384},{256,0},{384,128},{1,257},{129,385},{257,1},{385... | collective-permute-start | bytes 1179656 | tf_op jit(solution)/shard_map/ppermute | solution.py:149
  9.2 4.1 %collective-permute-start.9 = (bf16[64,3072]{1,0:T(8,128)(2,1)S(1)}, bf16[64,3072]{1,0:T(8,128)(2,1)S(1)}, u32[]{:S(2)}, u32[]{:S(2)}) collective-permute-start(bf16[64,3072]{1,0:T(8,128)(2,1)S(1)} %bitcast.30), channel_id=1, source_target_pairs={{0,384},{128,0},{256,128},{384,256},{1,385},{129,1},{257,129},{385... | collective-permute-start | bytes 1179656 | tf_op jit(solution)/shard_map/ppermute | solution.py:149
  13.3 2.9 %collective-permute-start.8 = (bf16[64,3072]{1,0:T(8,128)(2,1)S(1)}, bf16[64,3072]{1,0:T(8,128)(2,1)S(1)}, u32[]{:S(2)}, u32[]{:S(2)}) collective-permute-start(bf16[64,3072]{1,0:T(8,128)(2,1)S(1)} %bitcast.31), channel_id=1, source_target_pairs={{0,128},{128,256},{256,384},{384,0},{1,129},{129,257},{257,385},{3... | collective-permute-start | bytes 1179656 | tf_op jit(solution)/shard_map/ppermute | solution.py:149
  16.2 11.4 %collective-permute-start.1 = (bf16[64,3072]{1,0:T(8,128)(2,1)S(1)}, bf16[64,3072]{1,0:T(8,128)(2,1)S(1)}, u32[]{:S(2)}, u32[]{:S(2)}) collective-permute-start(bf16[64,3072]{1,0:T(8,128)(2,1)S(1)} %bitcast.32), channel_id=1, source_target_pairs={{1,0},{2,1},{3,2},{4,3},{5,4},{6,5},{7,6},{8,7},{9,8},{10,9},{11,1... | collective-permute-start | bytes 1179656 | tf_op jit(solution)/shard_map/ppermute | solution.py:31
  27.7 0.0 collective-permute-done.4.refs_0_
  27.7 1.9 %collective-permute-start = (bf16[64,3072]{1,0:T(8,128)(2,1)S(1)}, bf16[64,3072]{1,0:T(8,128)(2,1)S(1)}, u32[]{:S(2)}, u32[]{:S(2)}) collective-permute-start(bf16[64,3072]{1,0:T(8,128)(2,1)S(1)} %bitcast.33), channel_id=1, source_target_pairs={{0,1},{1,2},{2,3},{3,4},{4,5},{5,6},{6,7},{7,8},{8,9},{9,10},{10,1... | collective-permute-start | bytes 1179656 | tf_op jit(solution)/shard_map/ppermute | solution.py:31
  29.6 5.3 %collective-permute-done.1.after = bf16[64,3072]{1,0:T(8,128)(2,1)S(1)} collective-permute-done((bf16[64,3072]{1,0:T(8,128)(2,1)S(1)}, bf16[64,3072]{1,0:T(8,128)(2,1)S(1)}, u32[]{:S(2)}, u32[]{:S(2)}) %collective-permute-start.1) | collective-permute-done | bytes 393248 | tf_op jit(solution)/shard_map/ppermute | solution.py:31
  34.9 3.0 %collective-permute-start.7 = (bf16[64,3072]{1,0:T(8,128)(2,1)S(1)}, bf16[64,3072]{1,0:T(8,128)(2,1)S(1)}, u32[]{:S(2)}, u32[]{:S(2)}) collective-permute-start(bf16[64,3072]{1,0:T(8,128)(2,1)S(1)} %stack.18), channel_id=1, source_target_pairs={{0,256},{128,384},{256,0},{384,128},{1,257},{129,385},{257,1},{385... | collective-permute-start | bytes 1179656 | tf_op jit(solution)/shard_map/ppermute | solution.py:155
  37.9 3.2 %collective-permute-done.before = bf16[64,3072]{1,0:T(8,128)(2,1)S(1)} collective-permute-done((bf16[64,3072]{1,0:T(8,128)(2,1)S(1)}, bf16[64,3072]{1,0:T(8,128)(2,1)S(1)}, u32[]{:S(2)}, u32[]{:S(2)}) %collective-permute-start) | collective-permute-done | bytes 393248 | tf_op jit(solution)/shard_map/ppermute | solution.py:31
  41.1 1.9 %collective-permute-start.6 = (bf16[64,3072]{1,0:T(8,128)(2,1)S(1)}, bf16[64,3072]{1,0:T(8,128)(2,1)}, u32[]{:S(2)}, u32[]{:S(2)}) collective-permute-start(bf16[64,3072]{1,0:T(8,128)(2,1)S(1)} %stack.18), channel_id=1, source_target_pairs={{0,384},{128,0},{256,128},{384,256},{1,385},{129,1},{257,129},{385... | collective-permute-start | bytes 1179656 | tf_op jit(solution)/shard_map/ppermute | solution.py:155
  43.1 0.0 copy-done
  43.1 0.9 stencil_first.1.mid
  43.9 0.0 collective-permute-done.10.refs_3_
  43.9 5.1 %collective-permute-start.5 = (bf16[64,3072]{1,0:T(8,128)(2,1)S(1)}, bf16[64,3072]{1,0:T(8,128)(2,1)}, u32[]{:S(2)}, u32[]{:S(2)}) collective-permute-start(bf16[64,3072]{1,0:T(8,128)(2,1)S(1)} %stack.18), channel_id=1, source_target_pairs={{0,128},{128,256},{256,384},{384,0},{1,129},{129,257},{257,385},{3... | collective-permute-start | bytes 1179656 | tf_op jit(solution)/shard_map/ppermute | solution.py:155
  49.1 0.0 collective-permute-done.9.refs_2_
  49.1 3.3 %collective-permute-start.3 = (bf16[64,3072]{1,0:T(8,128)(2,1)S(1)}, bf16[64,3072]{1,0:T(8,128)(2,1)S(1)}, u32[]{:S(2)}, u32[]{:S(2)}) collective-permute-start(bf16[64,3072]{1,0:T(8,128)(2,1)S(1)} %stencil_first.1.mid), channel_id=1, source_target_pairs={{1,0},{2,1},{3,2},{4,3},{5,4},{6,5},{7,6},{8,7},{9,8},{10,9},{11,1... | collective-permute-start | bytes 1179656 | tf_op jit(solution)/shard_map/ppermute | solution.py:31
  52.4 0.0 collective-permute-done.8.refs_1_
  52.4 2.6 %collective-permute-start.2 = (bf16[64,3072]{1,0:T(8,128)(2,1)S(1)}, bf16[64,3072]{1,0:T(8,128)(2,1)S(1)}, u32[]{:S(2)}, u32[]{:S(2)}) collective-permute-start(bf16[64,3072]{1,0:T(8,128)(2,1)S(1)} %stencil_first.1.mid), channel_id=1, source_target_pairs={{0,1},{1,2},{2,3},{3,4},{4,5},{5,6},{6,7},{7,8},{8,9},{9,10},{10,1... | collective-permute-start | bytes 1179656 | tf_op jit(solution)/shard_map/ppermute | solution.py:31
  55.0 0.1 pad_add_fusion.place
  55.1 0.1 stack.19
  55.2 0.0 collective-permute-done.7
  55.2 1.9 %collective-permute-start.11 = (bf16[256,3072]{1,0:T(8,128)(2,1)S(1)}, bf16[256,3072]{1,0:T(8,128)(2,1)S(1)}, u32[]{:S(2)}, u32[]{:S(2)}) collective-permute-start(bf16[256,3072]{1,0:T(8,128)(2,1)S(1)} %stack.19), channel_id=1, source_target_pairs={{0,32},{32,0},{1,33},{33,1},{2,34},{34,2},{3,35},{35,3},{4,36},{36... | collective-permute-start | bytes 4718600 | tf_op jit(solution)/shard_map/ppermute | solution.py:138
  57.1 0.0 collective-permute-done.6
  57.1 0.0 collective-permute-done.5
  57.1 1.8 %collective-permute-done.3.after = bf16[64,3072]{1,0:T(8,128)(2,1)S(1)} collective-permute-done((bf16[64,3072]{1,0:T(8,128)(2,1)S(1)}, bf16[64,3072]{1,0:T(8,128)(2,1)S(1)}, u32[]{:S(2)}, u32[]{:S(2)}) %collective-permute-start.3) | collective-permute-done | bytes 393248 | tf_op jit(solution)/shard_map/ppermute | solution.py:31
  59.0 5.2 %collective-permute-done.2.before = bf16[64,3072]{1,0:T(8,128)(2,1)S(1)} collective-permute-done((bf16[64,3072]{1,0:T(8,128)(2,1)S(1)}, bf16[64,3072]{1,0:T(8,128)(2,1)S(1)}, u32[]{:S(2)}, u32[]{:S(2)}) %collective-permute-start.2) | collective-permute-done | bytes 393248 | tf_op jit(solution)/shard_map/ppermute | solution.py:31
  64.2 1.2 %pad_maximum_fusion = bf16[256,3072]{1,0:T(8,128)(2,1)S(1)} fusion(bf16[64,3072]{1,0:T(8,128)(2,1)S(1)} %collective-permute-done.7, bf16[64,3072]{1,0:T(8,128)(2,1)} %collective-permute-done.6, bf16[64,3072]{1,0:T(8,128)(2,1)} %collective-permute-done.5, bf16[64,3072]{1,0:T(8,128)(2,1)S(1)} %stack.18), kind=kLoop, calls=%fused_computation.3 | loop fusion | flops 6291456 | bytes 3145728 | tf_op jit(solution)/shard_map/concatenate | solution.py:163
  65.4 1.9 %collective-permute-start.12 = (bf16[256,3072]{1,0:T(8,128)(2,1)S(1)}, bf16[256,3072]{1,0:T(8,128)(2,1)S(1)}, u32[]{:S(2)}, u32[]{:S(2)}) collective-permute-start(bf16[256,3072]{1,0:T(8,128)(2,1)S(1)} %pad_maximum_fusion), channel_id=1, source_target_pairs={{0,32},{32,0},{1,33},{33,1},{2,34},{34,2},{3,35},{35,3},{4,36},{36... | collective-permute-start | bytes 4718600 | tf_op jit(solution)/shard_map/ppermute | solution.py:138
  67.3 0.9 stencil_second.1
  68.2 0.6 convolution_convert_fusion.3
  68.8 0.6 convolution_convert_fusion.1
  69.4 0.0 collective-permute-done.11
  69.4 0.6 convolution_convert_fusion.2
  70.0 0.0 copy-start.1
  70.0 0.7 collective-permute-done.12
  70.7 0.6 convolution_convert_fusion
  71.3 10.2 %all_to_all.15.pieces = bf16[8,8,1024]{2,1,0:T(8,128)(2,1)S(1)} all-to-all(bf16[8,8,1024]{2,1,0:T(8,128)(2,1)S(1)} %maximum_bitcast_fusion), channel_id=1, replica_groups=mesh['y'=4,'xh'=2,'core'=2,'xl'=2,'z1'=4,'z0'=4] {'xl','z0'}, dimensions={0} | all-to-all | bytes 262144 | tf_op jit(solution)/shard_map/all_to_all | solution.py:173
  81.5 16.9 %all_to_all.16.pieces = bf16[4,8,1024]{2,1,0:T(8,128)(2,1)S(1)} all-to-all(bf16[4,8,1024]{2,1,0:T(8,128)(2,1)S(1)} %share.1), channel_id=1, replica_groups=mesh['y'=4,'xh'=2,'core'=2,'xl'=2,'z1'=4,'z0'=4] {'z1'}, dimensions={0} | all-to-all | bytes 131072 | tf_op jit(solution)/shard_map/all_to_all | solution.py:183
  98.4 0.6 coef.1
  99.0 9.9 %all_to_all.17 = bf16[8,8,1024]{2,1,0:T(8,128)(2,1)S(1)} all-to-all(bf16[8,8,1024]{2,1,0:T(8,128)(2,1)S(1)} %coef.1), channel_id=1, replica_groups=mesh['y'=4,'xh'=2,'core'=2,'xl'=2,'z1'=4,'z0'=4] {'xl','z0'}, dimensions={0} | all-to-all | bytes 262144 | tf_op jit(solution)/shard_map/all_to_all | solution.py:192
  109.0 0.4 fusion.3
  109.3 0.4 fusion.7
  109.7 0.4 fusion.5
  110.1 0.5 fusion.2
  110.6 0.8 copy.5
  (4 shorter events, 0.1 us)
Async XLA Ops:
  1.1 42.0 %copy-start = (f32[3,8,128]{2,1,0:T(8,128)S(1)}, f32[3,8,128]{2,1,0:T(8,128)}, u32[]{:S(2)}) copy-start(f32[3,8,128]{2,1,0:T(8,128)} %param.4) | copy-start | bytes 36868
  1.1 26.6 %collective-permute-start.4 = (bf16[64,3072]{1,0:T(8,128)(2,1)S(1)}, bf16[64,3072]{1,0:T(8,128)(2,1)S(1)}, u32[]{:S(2)}, u32[]{:S(2)}) collective-permute-start(bf16[64,3072]{1,0:T(8,128)(2,1)S(1)} %bitcast.28), channel_id=1, source_target_pairs={{0,64},{64,0},{1,65},{65,1},{2,66},{66,2},{3,67},{67,3},{4,68},{68... | collective-permute-start | bytes 1179656 | tf_op jit(solution)/shard_map/ppermute | solution.py:138
  6.0 37.9 %collective-permute-start.10 = (bf16[64,3072]{1,0:T(8,128)(2,1)S(1)}, bf16[64,3072]{1,0:T(8,128)(2,1)S(1)}, u32[]{:S(2)}, u32[]{:S(2)}) collective-permute-start(bf16[64,3072]{1,0:T(8,128)(2,1)S(1)} %bitcast.29), channel_id=1, source_target_pairs={{0,256},{128,384},{256,0},{384,128},{1,257},{129,385},{257,1},{385... | collective-permute-start | bytes 1179656 | tf_op jit(solution)/shard_map/ppermute | solution.py:149
  9.2 39.9 %collective-permute-start.9 = (bf16[64,3072]{1,0:T(8,128)(2,1)S(1)}, bf16[64,3072]{1,0:T(8,128)(2,1)S(1)}, u32[]{:S(2)}, u32[]{:S(2)}) collective-permute-start(bf16[64,3072]{1,0:T(8,128)(2,1)S(1)} %bitcast.30), channel_id=1, source_target_pairs={{0,384},{128,0},{256,128},{384,256},{1,385},{129,1},{257,129},{385... | collective-permute-start | bytes 1179656 | tf_op jit(solution)/shard_map/ppermute | solution.py:149
  13.3 39.1 %collective-permute-start.8 = (bf16[64,3072]{1,0:T(8,128)(2,1)S(1)}, bf16[64,3072]{1,0:T(8,128)(2,1)S(1)}, u32[]{:S(2)}, u32[]{:S(2)}) collective-permute-start(bf16[64,3072]{1,0:T(8,128)(2,1)S(1)} %bitcast.31), channel_id=1, source_target_pairs={{0,128},{128,256},{256,384},{384,0},{1,129},{129,257},{257,385},{3... | collective-permute-start | bytes 1179656 | tf_op jit(solution)/shard_map/ppermute | solution.py:149
  16.2 18.7 %collective-permute-start.1 = (bf16[64,3072]{1,0:T(8,128)(2,1)S(1)}, bf16[64,3072]{1,0:T(8,128)(2,1)S(1)}, u32[]{:S(2)}, u32[]{:S(2)}) collective-permute-start(bf16[64,3072]{1,0:T(8,128)(2,1)S(1)} %bitcast.32), channel_id=1, source_target_pairs={{1,0},{2,1},{3,2},{4,3},{5,4},{6,5},{7,6},{8,7},{9,8},{10,9},{11,1... | collective-permute-start | bytes 1179656 | tf_op jit(solution)/shard_map/ppermute | solution.py:31
  27.7 13.5 %collective-permute-start = (bf16[64,3072]{1,0:T(8,128)(2,1)S(1)}, bf16[64,3072]{1,0:T(8,128)(2,1)S(1)}, u32[]{:S(2)}, u32[]{:S(2)}) collective-permute-start(bf16[64,3072]{1,0:T(8,128)(2,1)S(1)} %bitcast.33), channel_id=1, source_target_pairs={{0,1},{1,2},{2,3},{3,4},{4,5},{5,6},{6,7},{7,8},{8,9},{9,10},{10,1... | collective-permute-start | bytes 1179656 | tf_op jit(solution)/shard_map/ppermute | solution.py:31
  34.9 20.3 %collective-permute-start.7 = (bf16[64,3072]{1,0:T(8,128)(2,1)S(1)}, bf16[64,3072]{1,0:T(8,128)(2,1)S(1)}, u32[]{:S(2)}, u32[]{:S(2)}) collective-permute-start(bf16[64,3072]{1,0:T(8,128)(2,1)S(1)} %stack.18), channel_id=1, source_target_pairs={{0,256},{128,384},{256,0},{384,128},{1,257},{129,385},{257,1},{385... | collective-permute-start | bytes 1179656 | tf_op jit(solution)/shard_map/ppermute | solution.py:155
  41.1 16.0 %collective-permute-start.6 = (bf16[64,3072]{1,0:T(8,128)(2,1)S(1)}, bf16[64,3072]{1,0:T(8,128)(2,1)}, u32[]{:S(2)}, u32[]{:S(2)}) collective-permute-start(bf16[64,3072]{1,0:T(8,128)(2,1)S(1)} %stack.18), channel_id=1, source_target_pairs={{0,384},{128,0},{256,128},{384,256},{1,385},{129,1},{257,129},{385... | collective-permute-start | bytes 1179656 | tf_op jit(solution)/shard_map/ppermute | solution.py:155
  43.9 13.2 %collective-permute-start.5 = (bf16[64,3072]{1,0:T(8,128)(2,1)S(1)}, bf16[64,3072]{1,0:T(8,128)(2,1)}, u32[]{:S(2)}, u32[]{:S(2)}) collective-permute-start(bf16[64,3072]{1,0:T(8,128)(2,1)S(1)} %stack.18), channel_id=1, source_target_pairs={{0,128},{128,256},{256,384},{384,0},{1,129},{129,257},{257,385},{3... | collective-permute-start | bytes 1179656 | tf_op jit(solution)/shard_map/ppermute | solution.py:155
  49.1 9.9 %collective-permute-start.3 = (bf16[64,3072]{1,0:T(8,128)(2,1)S(1)}, bf16[64,3072]{1,0:T(8,128)(2,1)S(1)}, u32[]{:S(2)}, u32[]{:S(2)}) collective-permute-start(bf16[64,3072]{1,0:T(8,128)(2,1)S(1)} %stencil_first.1.mid), channel_id=1, source_target_pairs={{1,0},{2,1},{3,2},{4,3},{5,4},{6,5},{7,6},{8,7},{9,8},{10,9},{11,1... | collective-permute-start | bytes 1179656 | tf_op jit(solution)/shard_map/ppermute | solution.py:31
  52.4 11.8 %collective-permute-start.2 = (bf16[64,3072]{1,0:T(8,128)(2,1)S(1)}, bf16[64,3072]{1,0:T(8,128)(2,1)S(1)}, u32[]{:S(2)}, u32[]{:S(2)}) collective-permute-start(bf16[64,3072]{1,0:T(8,128)(2,1)S(1)} %stencil_first.1.mid), channel_id=1, source_target_pairs={{0,1},{1,2},{2,3},{3,4},{4,5},{5,6},{6,7},{7,8},{8,9},{9,10},{10,1... | collective-permute-start | bytes 1179656 | tf_op jit(solution)/shard_map/ppermute | solution.py:31
  55.2 14.2 %collective-permute-start.11 = (bf16[256,3072]{1,0:T(8,128)(2,1)S(1)}, bf16[256,3072]{1,0:T(8,128)(2,1)S(1)}, u32[]{:S(2)}, u32[]{:S(2)}) collective-permute-start(bf16[256,3072]{1,0:T(8,128)(2,1)S(1)} %stack.19), channel_id=1, source_target_pairs={{0,32},{32,0},{1,33},{33,1},{2,34},{34,2},{3,35},{35,3},{4,36},{36... | collective-permute-start | bytes 4718600 | tf_op jit(solution)/shard_map/ppermute | solution.py:138
  65.4 5.3 %collective-permute-start.12 = (bf16[256,3072]{1,0:T(8,128)(2,1)S(1)}, bf16[256,3072]{1,0:T(8,128)(2,1)S(1)}, u32[]{:S(2)}, u32[]{:S(2)}) collective-permute-start(bf16[256,3072]{1,0:T(8,128)(2,1)S(1)} %pad_maximum_fusion), channel_id=1, source_target_pairs={{0,32},{32,0},{1,33},{33,1},{2,34},{34,2},{3,35},{35,3},{4,36},{36... | collective-permute-start | bytes 4718600 | tf_op jit(solution)/shard_map/ppermute | solution.py:138
  70.0 28.4 %copy-start.1 = (s32[16]{0:T(128)S(1)}, s32[16]{0:T(128)}, u32[]{:S(2)}) copy-start(s32[16]{0:T(128)} %plan.1) | copy-start | bytes 196
